TPU v7x, 128 devices: a whole 4x4x4 slice. The times are simulated.
128 devices in a mesh: gx: 8 (over z, core), gy: 16 (over x, y).
Axes of the slice: x: 4, y: 4, z: 4, core: 2. Of those that a mesh axis runs over, the one named last changes fastest.
Arguments:
- gaseous_rho: float32 [16, 1536, 1024], P(None, 'gy', 'gx'), may hold values from 0.5 to 2
- gaseous_flow_vector: float32 [3, 16, 1536, 1024], P(None, None, 'gy', 'gx'), may hold values from -1 to 1
- gaseous_kelvin: float32 [16, 1536, 1024], P(None, 'gy', 'gx'), may hold values from 0.5 to 2
- sender_tile_map: int32 [128, 256], P(('gx', 'gy')), may hold values from -1 to 1535, as said below
- receiver_arrival_rank: int32 [8192], P(('gx', 'gy')), may hold values from -1 to 255, as said below
- bin_active_number: int32 [8192], P(('gx', 'gy')), may hold values from 0 to 512, as said below
- grain_inertia: float32 [8192, 512], P(('gx', 'gy')), may hold values from 0.05 to 0.5
- grain_motion_vector: float32 [3, 8192, 512], P(None, ('gx', 'gy')), may hold values from -5 to 5
- grain_kelvin: float32 [8192, 512], P(('gx', 'gy')), may hold values from 0.5 to 4
- grain_voxel_number: int32 [8192, 512], P(('gx', 'gy')), may hold values from 0 to 127
- grain_substance_label: int32 [8192, 512], P(('gx', 'gy')), may hold values from 0 to 1
- exchange_factor: float32 [2, 2], replicated, may hold values from 0.5 to 4
Outputs:
- gas_state_out: float32 [5, 16, 1536, 1024], P(None, None, 'gy', 'gx')
- solid_state: float32 [4, 8192, 2, 128], P(None, ('gx', 'gy'))
Inputs may be any that keep to these rules, and one draw needn't show every extreme that they name: sender_tile_map[s, o * 2 + r] is the local block that device s sends as its r-th block to owner o, -1 where it sends fewer; the blocks of one device are distinct; only 32 devices send, each to every owner. `receiver_arrival_rank`: an owner's live slots come first, 48 or more of them, and name each sent block of that owner once; in each draw some owner has all 64 live and receives exactly 2 blocks from each sending device. `bin_active_number`: 0 exactly on slots with receiver_arrival_rank -1, else 512 // 2 or more; some slot holds 512.
All inputs are finite; a program needn't handle non-finite values.
Results may differ from a plain program's by a relative error of at most 0.0003.
Values sent between devices are 32-bit elements; how exact they have to be, the bound alone decides.
No kernel may reach another device: no remote copies, remote signals or barrier semaphores. Data moves between devices by JAX's collectives and lax.ppermute only.
A program may use at most 128 MiB of HBM per device.

v0:
```python
import functools
import jax
import jax.numpy as jnp
from jax import lax
from jax.experimental import pallas as pl
from jax.experimental.pallas import tpu as pltpu
from jax.sharding import PartitionSpec as P

step_ratio = 0.08
fields = 5
lanes = 128
row_pad = 8
block_rows = 12
gas_row = 6
row_chunk = 16

VM = pltpu.VMEM
vmem_spec = pl.BlockSpec(memory_space=pltpu.VMEM)
smem_spec = pl.BlockSpec(memory_space=pltpu.SMEM)
any_spec = pl.BlockSpec(memory_space=pl.ANY)


def params(mib):
    return pltpu.CompilerParams(vmem_limit_bytes=mib * 1024 * 1024)


def struct(*shape):
    return jax.ShapeDtypeStruct(shape, jnp.float32)


def lane_index(shape):
    return lax.broadcasted_iota(jnp.int32, shape, len(shape) - 1)


def edges_kernel(rho, flow, kelvin, left, right, low, high, held, sems):
    depth, height, _ = rho.shape
    parts = sems.shape[1]
    rows = height // parts

    def copies(part):
        span = pl.ds(part * rows, rows)
        return [
            pltpu.make_async_copy(rho.at[:, span], held.at[0, :, span], sems.at[0, part]),
            pltpu.make_async_copy(flow.at[:, :, span], held.at[1:4, :, span], sems.at[1, part]),
            pltpu.make_async_copy(kelvin.at[:, span], held.at[4, :, span], sems.at[2, part]),
        ]

    for part in range(parts):
        for copy in copies(part):
            copy.start()
    lane = lane_index((8, lanes))
    for part in range(parts):
        for copy in copies(part):
            copy.wait()

        def group(g, carry):
            start = pl.multiple_of(part * rows + g * 8, 8)
            span = pl.ds(start, 8)
            first = jnp.zeros((8, lanes), jnp.float32)
            last = jnp.zeros((8, lanes), jnp.float32)
            for f in range(fields):
                for z in range(depth):
                    k = f * depth + z
                    turned = pltpu.roll(held[f, z, span, :], k + 1, 1)
                    last = jnp.where(lane == k, turned, last)
                    first = jnp.where(lane == k + 1, turned, first)
            left[span, :] = pltpu.roll(first, lanes - 1, 1)
            right[span, :] = last
            return carry

        lax.fori_loop(0, rows // 8, group, 0)
    for f in range(fields):
        for z in range(depth):
            k = f * depth + z
            low[k : k + 1, :] = held[f, z, 0:1, :]
            high[k : k + 1, :] = held[f, z, height - 1 : height, :]


def edges(rho, flow, kelvin):
    depth, height, width = rho.shape
    parts = 4
    return pl.pallas_call(
        edges_kernel,
        out_shape=(
            struct(height, width),
            struct(height, width),
            struct(fields * depth, width),
            struct(fields * depth, width),
        ),
        in_specs=[any_spec] * 3,
        out_specs=(vmem_spec,) * 4,
        scratch_shapes=[
            VM((fields, depth, height, width), jnp.float32),
            pltpu.SemaphoreType.DMA((3, parts)),
        ],
        compiler_params=params(24),
        name="edges",
    )(rho, flow, kelvin)


def binning_kernel(count, factor, mass, flow, kelvin, cell, label, shared, solid, held, sums):
    slots, padding = mass.shape
    width = lanes

    def group(g, carry):
        span = pl.ds(pl.multiple_of(g * 8, 8), 8)
        base = pl.multiple_of(g * 64, 64)
        for part in range(padding // lanes):
            chunk = pl.ds(part * lanes, lanes)
            m = mass[span, chunk]
            values = [m] + [m * flow[c, span, chunk] for c in range(3)] + [m * kelvin[span, chunk]]
            values = values + [jnp.zeros_like(m)] * 3
            for c in range(8):
                held[part, pl.ds(base + c, 8, stride=8), :] = values[c]
        return carry

    lax.fori_loop(0, slots // 8, group, 0)
    place = lane_index((1, padding))
    columns = lax.broadcasted_iota(jnp.int32, (width, padding), 0)

    def slot_sums(s, carry):
        row = pl.ds(pl.multiple_of(s * 8, 8), 8)
        base = jnp.concatenate([held[part, row, :] for part in range(padding // lanes)], 1)
        target = jnp.where(place < count[s], cell[pl.ds(s, 1), :], -1)
        kind = label[pl.ds(s, 1), :]
        table = jnp.where(columns == target, 1.0, 0.0).astype(jnp.bfloat16)
        both = jnp.concatenate(
            [jnp.where(kind == 0, base, 0.0), jnp.where(kind == 1, base, 0.0)], 0
        )
        coarse = both.astype(jnp.bfloat16)
        fine = (both - coarse.astype(jnp.float32)).astype(jnp.bfloat16)
        summed = lax.dot_general(
            jnp.concatenate([coarse, fine], 0),
            table,
            (((1,), (1,)), ((), ())),
            preferred_element_type=jnp.float32,
        )
        sums[pl.ds(pl.multiple_of(s * 16, 16), 16), :] = summed[0:16] + summed[16:32]
        return carry

    lax.fori_loop(0, slots, slot_sums, 0, unroll=4)
    totals = [0.0] * 6
    for m in range(2):
        drag, thermal = factor[m, 0], factor[m, 1]

        def row(c):
            return sums[pl.ds(8 * m + c, slots, stride=16), :]

        inertia = row(0)
        by_drag = 1.0 / (inertia + drag)
        by_heat = 1.0 / (inertia + thermal)
        for c in range(3):
            scaled = row(1 + c) * by_drag
            solid[(m * 6 + c) * slots : (m * 6 + c + 1) * slots, :] = scaled
            totals[c] = totals[c] + drag * scaled
        scaled = row(4) * by_heat
        solid[(m * 6 + 3) * slots : (m * 6 + 4) * slots, :] = scaled
        totals[3] = totals[3] + thermal * scaled
        by_drag = drag * by_drag
        by_heat = thermal * by_heat
        solid[(m * 6 + 4) * slots : (m * 6 + 5) * slots, :] = by_drag
        solid[(m * 6 + 5) * slots : (m * 6 + 6) * slots, :] = by_heat
        totals[4] = totals[4] + by_drag * inertia
        totals[5] = totals[5] + by_heat * inertia
    for c in range(6):
        shared[c * slots : (c + 1) * slots, :] = totals[c]


def binning(count, factor, mass, flow, kelvin, cell, label):
    slots, padding = mass.shape
    return pl.pallas_call(
        binning_kernel,
        out_shape=(struct(6 * slots, lanes), struct(12 * slots, lanes)),
        in_specs=[smem_spec] * 2 + [vmem_spec] * 5,
        out_specs=(vmem_spec,) * 2,
        scratch_shapes=[
            VM((padding // lanes, slots * 8, lanes), jnp.float32),
            VM((slots * 16, lanes), jnp.float32),
        ],
        cost_estimate=pl.CostEstimate(
            flops=4_000_000_000, bytes_accessed=12_000_000, transcendentals=0
        ),
        compiler_params=params(16),
        name="binning",
    )(count, factor, mass, flow, kelvin, cell, label)


def fluxes(a, b, normal, keep=None):
    speed = (0.5 * step_ratio) * (a[normal] + b[normal]) - (2.0 * step_ratio * step_ratio) * (
        b[0] * b[4] - a[0] * a[4]
    ) / (a[0] + b[0])
    if keep is not None:
        speed = speed * keep
    ahead = speed > 0
    chosen = [jnp.where(ahead, u, v) for u, v in zip(a, b)]
    through = speed * chosen[0]
    return [through] + [through * c for c in chosen[1:]]


def advect_kernel(
    tiles,
    rank,
    rho,
    flow,
    kelvin,
    own_left,
    own_right,
    from_left,
    from_right,
    from_low,
    from_high,
    shared,
    gas_out,
    send_out,
    state,
    gas,
    send,
    flux_z,
    flux_y,
    side,
    in_sems,
    out_sems,
    send_sem,
):
    depth, height, width = rho.shape
    cells = depth * height
    slots = rank.shape[0]
    gx, gy = lax.axis_index("gx"), lax.axis_index("gy")

    def keep(wall):
        return jnp.where(wall, 0.0, 1.0).astype(jnp.float32)

    keep_left = keep(gx == 0)
    keep_right = keep(gx == lax.axis_size("gx") - 1)
    keep_low = keep(gy == 0)
    keep_high = keep(gy == lax.axis_size("gy") - 1)
    inner = pl.ds(row_pad, height)

    def loads(z):
        return [
            pltpu.make_async_copy(rho.at[z], state.at[0, z, inner], in_sems.at[0, z]),
            pltpu.make_async_copy(flow.at[:, z], state.at[1:4, z, inner], in_sems.at[1, z]),
            pltpu.make_async_copy(kelvin.at[z], state.at[4, z, inner], in_sems.at[2, z]),
        ]

    def store(z):
        rows = pl.ds(pl.multiple_of(z * height, 8), height)
        return pltpu.make_async_copy(gas.at[:, rows], gas_out.at[:, z], out_sems.at[z])

    def start_loads(z, carry):
        for copy in loads(z):
            copy.start()
        return carry

    lax.fori_loop(0, depth, start_loads, 0)

    def boundary(g, carry):
        span = pl.ds(pl.multiple_of(g * 8, 8), 8)

        def split(ref):
            packed = ref[span, :]
            return [packed] + [
                pltpu.roll(packed, lanes - f * depth, 1) for f in range(1, fields)
            ]

        lower = fluxes(split(from_left), split(own_left), 1, keep_left)
        upper = fluxes(split(own_right), split(from_right), 1, keep_right)
        for f in range(fields):
            side[f, span, :] = lower[f]
            side[fields + f, span, :] = upper[f]
        return carry

    lax.fori_loop(0, height // 8, boundary, 0)

    for f in range(fields):
        flux_z[f] = jnp.zeros((height, width), jnp.float32)
    for copy in loads(0):
        copy.wait()
    lane = lane_index((row_chunk, lanes))

    def plane(z, carry):
        above = jnp.minimum(z + 1, depth - 1)

        @pl.when(z + 1 < depth)
        def _():
            for copy in loads(above):
                copy.wait()

        keep_z = keep(z + 1 == depth)
        for f in range(fields):
            k = f * depth + z
            state[f, z, row_pad - 1 : row_pad, :] = from_low[pl.ds(k, 1), :]
            state[f, z, row_pad + height : row_pad + height + 1, :] = from_high[pl.ds(k, 1), :]

        def faces_y(start, rows):
            a = [state[f, z, pl.ds(row_pad - 1 + start, rows), :] for f in range(fields)]
            b = [state[f, z, pl.ds(row_pad + start, rows), :] for f in range(fields)]
            for f, value in enumerate(fluxes(a, b, 2)):
                flux_y[f, start : start + rows, :] = value

        for start in range(0, height, row_chunk):
            faces_y(start, row_chunk)
        faces_y(height, 1)
        for f in range(fields):
            flux_y[f, 0:1, :] = flux_y[f, 0:1, :] * keep_low
            flux_y[f, height : height + 1, :] = flux_y[f, height : height + 1, :] * keep_high

        for start in range(0, height, row_chunk):
            span = pl.ds(start, row_chunk)
            here = [state[f, z, pl.ds(row_pad + start, row_chunk), :] for f in range(fields)]
            over = [state[f, above, pl.ds(row_pad + start, row_chunk), :] for f in range(fields)]
            up = fluxes(here, over, 3, keep_z)
            change = []
            for f in range(fields):
                change.append(
                    (up[f] - flux_z[f, span, :])
                    + (flux_y[f, pl.ds(start + 1, row_chunk), :] - flux_y[f, span, :])
                )
                flux_z[f, span, :] = up[f]
            before = [pltpu.roll(h, 1, 1) for h in here]
            faces = fluxes(before, here, 1)
            for f in range(fields):
                lower = pltpu.roll(side[f, span, :], lanes - z, 1)
                upper = pltpu.roll(side[fields + f, span, :], lanes - 1 - z, 1)
                face = jnp.where(lane == 0, lower, faces[f])
                after = jnp.where(lane == lanes - 1, upper, pltpu.roll(face, lanes - 1, 1))
                change[f] = change[f] + (after - face)
            density = here[0] - change[0]
            inverse = 1.0 / density
            rows = pl.ds(pl.multiple_of(z * height + start, 8), row_chunk)
            gas[0, rows, :] = density
            for f in range(1, fields):
                gas[f, rows, :] = (here[0] * here[f] - change[f]) * inverse
        store(z).start()
        return carry

    lax.fori_loop(0, depth, plane, 0)

    total = tiles.shape[1]

    def pack_gas(i, carry):
        block = jnp.maximum(tiles[0, i], 0)
        for f in range(fields):
            send[pl.ds(i * block_rows + gas_row + f, 1), :] = gas[f, pl.ds(block, 1), :]
        return carry

    lax.fori_loop(0, total, pack_gas, 0, unroll=8)

    def pack_shared(k, carry):
        where_to = rank[k]
        row = jnp.where(where_to >= 0, where_to, total) * block_rows
        for c in range(6):
            send[pl.ds(row + c, 1), :] = shared[pl.ds(c * slots + k, 1), :]
        return carry

    lax.fori_loop(0, slots, pack_shared, 0, unroll=4)
    copy = pltpu.make_async_copy(send.at[pl.ds(0, total * block_rows)], send_out, send_sem)
    copy.start()

    def finish(z, carry):
        store(z).wait()
        return carry

    lax.fori_loop(0, depth, finish, 0)
    copy.wait()


def advect(tiles, rank, rho, flow, kelvin, own, received, shared):
    depth, height, width = rho.shape
    total = tiles.shape[1]
    return pl.pallas_call(
        advect_kernel,
        out_shape=(
            struct(fields, depth, height, width),
            struct(total * block_rows, width),
        ),
        in_specs=[smem_spec] * 2 + [any_spec] * 3 + [vmem_spec] * 7,
        out_specs=(any_spec,) * 2,
        scratch_shapes=[
            VM((fields, depth, height + 2 * row_pad, width), jnp.float32),
            VM((fields, depth * height, width), jnp.float32),
            VM(((total + 2) * block_rows, width), jnp.float32),
            VM((fields, height, width), jnp.float32),
            VM((fields, height + row_pad, width), jnp.float32),
            VM((2 * fields, height, width), jnp.float32),
            pltpu.SemaphoreType.DMA((3, depth)),
            pltpu.SemaphoreType.DMA((depth,)),
            pltpu.SemaphoreType.DMA,
        ],
        cost_estimate=pl.CostEstimate(
            flops=4_000_000_000, bytes_accessed=12_000_000, transcendentals=0
        ),
        compiler_params=params(32),
        name="advect",
    )(tiles, rank, rho, flow, kelvin, *own, *received, shared)


def mixed(density, gas, sums):
    by_flow = 1.0 / (density + sums[4])
    by_heat = 1.0 / (density + sums[5])
    flow = [(density * gas[c] + sums[c]) * by_flow for c in range(3)]
    return flow + [(density * gas[3] + sums[3]) * by_heat]


def exchange_kernel(
    tiles,
    rank,
    received,
    sent,
    advanced,
    shared,
    solid,
    gas_out,
    solid_out,
    gas,
    fresh,
    slot_gas,
    in_sems,
    out_sems,
):
    _, depth, height, width = advanced.shape
    cells = depth * height
    total = tiles.shape[1]
    slots = rank.shape[0]

    def load(f):
        return pltpu.make_async_copy(
            advanced.at[f], gas.at[f, pl.ds(0, depth)], in_sems.at[f]
        )

    for f in range(fields):
        load(f).start()

    def store(f):
        return pltpu.make_async_copy(
            gas.at[f, pl.ds(0, depth)], gas_out.at[f], out_sems.at[f]
        )

    def gather(k, live):
        spot = rank[k]
        row = jnp.maximum(spot, 0) * block_rows + gas_row
        for f in range(fields):
            slot_gas[f, pl.ds(k, 1), :] = received[pl.ds(row + f, 1), :]
        return live + jnp.where(spot >= 0, 1, 0)

    live = lax.fori_loop(0, slots, gather, 0, unroll=4)

    part = 32

    def blocks(g, carry):
        first = pl.multiple_of(g * part, part)

        def rows(ref, c):
            return ref[pl.ds(first * block_rows + c, part, stride=block_rows), :]

        result = mixed(
            rows(sent, gas_row),
            [rows(sent, gas_row + 1 + c) for c in range(4)],
            [rows(received, c) for c in range(6)],
        )
        for c in range(4):
            fresh[c, pl.ds(first, part), :] = result[c]
        return carry

    lax.fori_loop(0, total // part, blocks, 0)
    for f in range(fields):
        load(f).wait()
    store(0).start()

    def scatter(i, carry):
        block = tiles[0, i]
        block = jnp.where(block >= 0, block, cells)
        z = block // height
        y = block - z * height
        for c in range(4):
            gas[1 + c, z, pl.ds(y, 1), :] = fresh[c, pl.ds(i, 1), :]
        return carry

    lax.fori_loop(0, total, scatter, 0, unroll=8)
    for f in range(1, fields):
        store(f).start()

    result = mixed(
        slot_gas[0],
        [slot_gas[1 + c] for c in range(4)],
        [shared[c * slots : (c + 1) * slots, :] for c in range(6)],
    )
    alive = lax.broadcasted_iota(jnp.int32, (slots, width), 0) < live
    for m in range(2):
        for c in range(4):
            scale = solid[(m * 6 + 4 + c // 3) * slots : (m * 6 + 5 + c // 3) * slots, :]
            base = solid[(m * 6 + c) * slots : (m * 6 + c + 1) * slots, :]
            solid_out[c, pl.ds(m, slots, stride=2), :] = jnp.where(
                alive, base + scale * result[c], 0.0
            )
    for f in range(fields):
        store(f).wait()


def exchange(tiles, rank, received, sent, advanced, shared, solid):
    _, depth, height, width = advanced.shape
    total = tiles.shape[1]
    slots = rank.shape[0]
    return pl.pallas_call(
        exchange_kernel,
        out_shape=(struct(*advanced.shape), struct(4, 2 * slots, width)),
        in_specs=[smem_spec] * 2 + [vmem_spec] * 2 + [any_spec] + [vmem_spec] * 2,
        out_specs=(any_spec, vmem_spec),
        scratch_shapes=[
            VM((fields, depth + 1, height, width), jnp.float32),
            VM((4, total, width), jnp.float32),
            VM((fields, slots, width), jnp.float32),
            pltpu.SemaphoreType.DMA((fields,)),
            pltpu.SemaphoreType.DMA((fields,)),
        ],
        compiler_params=params(32),
        name="exchange",
    )(tiles, rank, received, sent, advanced, shared, solid)


def per_device(
    gaseous_rho,
    gaseous_flow_vector,
    gaseous_kelvin,
    sender_tile_map,
    receiver_arrival_rank,
    bin_active_number,
    grain_inertia,
    grain_motion_vector,
    grain_kelvin,
    grain_voxel_number,
    grain_substance_label,
    exchange_factor,
):
    left, right, low, high = edges(gaseous_rho, gaseous_flow_vector, gaseous_kelvin)

    def shifted(array, axis, step):
        count = lax.axis_size(axis)
        pairs = [(i, i + step) for i in range(count) if 0 <= i + step < count]
        return lax.ppermute(array, axis, pairs)

    received = (
        shifted(right, "gx", 1),
        shifted(left, "gx", -1),
        shifted(high, "gy", 1),
        shifted(low, "gy", -1),
    )
    shared, solid = binning(
        bin_active_number,
        exchange_factor,
        grain_inertia,
        grain_motion_vector,
        grain_kelvin,
        grain_voxel_number,
        grain_substance_label,
    )
    advanced, send = advect(
        sender_tile_map,
        receiver_arrival_rank,
        gaseous_rho,
        gaseous_flow_vector,
        gaseous_kelvin,
        (left, right),
        received,
        shared,
    )
    devices = lax.axis_size("gx") * lax.axis_size("gy")
    width = send.shape[-1]
    arrived = lax.all_to_all(
        send.reshape(devices, -1, width), ("gx", "gy"), split_axis=0, concat_axis=0, tiled=True
    )
    gas_state, solid_state = exchange(
        sender_tile_map,
        receiver_arrival_rank,
        arrived.reshape(-1, width),
        send,
        advanced,
        shared,
        solid,
    )
    return gas_state, solid_state.reshape(4, -1, 2, width)


def solution(mesh):
    placed = (
        P(None, "gy", "gx"),
        P(None, None, "gy", "gx"),
        P(None, "gy", "gx"),
        P(("gx", "gy"), None),
        P(("gx", "gy")),
        P(("gx", "gy")),
        P(("gx", "gy"), None),
        P(None, ("gx", "gy"), None),
        P(("gx", "gy"), None),
        P(("gx", "gy"), None),
        P(("gx", "gy"), None),
        P(),
    )
    return jax.shard_map(
        per_device,
        mesh=mesh,
        in_specs=placed,
        out_specs=(P(None, None, "gy", "gx"), P(None, ("gx", "gy"), None, None)),
        check_vma=False,
    )
```

profile of v0, /device:TPU:0, one launch (start us, length us, event | category | flops | bytes accessed | tf_op | source)
XLA Modules:
  0.0 90.5 jit_solution(5202012977473675595)
XLA Ops:
  0.6 0.0 copy-start
  0.6 1.7 %copy-done = f32[3,16,96,128]{3,2,1,0:T(8,128)S(1)} copy-done((f32[3,16,96,128]{3,2,1,0:T(8,128)S(1)}, f32[3,16,96,128]{3,2,1,0:T(8,128)}, u32[]{:S(2)}) %copy-start) | copy-done | bytes 2359320
  2.3 0.0 copy-start.2
  2.3 1.1 %copy-done.2 = f32[16,96,128]{2,1,0:T(8,128)S(1)} copy-done((f32[16,96,128]{2,1,0:T(8,128)S(1)}, f32[16,96,128]{2,1,0:T(8,128)}, u32[]{:S(2)}) %copy-start.2) | copy-done | bytes 786456
  3.4 0.0 copy-start.4
  3.4 1.1 %copy-done.4 = f32[16,96,128]{2,1,0:T(8,128)S(1)} copy-done((f32[16,96,128]{2,1,0:T(8,128)S(1)}, f32[16,96,128]{2,1,0:T(8,128)}, u32[]{:S(2)}) %copy-start.4) | copy-done | bytes 786456
  4.6 0.0 copy-start.8
  4.6 0.0 copy-start.9
  4.6 0.0 copy-start.10
  4.6 0.0 copy-start.11
  4.6 0.0 copy-start.12
  4.6 0.0 copy-start.13
  4.6 0.0 copy-start.14
  4.6 3.2 %edges.1 = (f32[96,128]{1,0:T(8,128)S(1)}, f32[96,128]{1,0:T(8,128)S(1)}, f32[80,128]{1,0:T(8,128)S(1)}, f32[80,128]{1,0:T(8,128)S(1)}) custom-call(f32[16,96,128]{2,1,0:T(8,128)S(1)} %copy-done.2, f32[3,16,96,128]{3,2,1,0:T(8,128)S(1)} %copy-done, f32[16,96,128]{2,1,0:T(8,128)S(1)} %copy-done.4), custom_call_target="tpu_custom_call" | custom-call | tf_op jit(solution)/shard_map/edges/pallas_call | solution.py:82
  7.8 3.6 %collective-permute-start.2 = (f32[80,128]{1,0:T(8,128)S(1)}, f32[80,128]{1,0:T(8,128)S(1)}, u32[]{:S(2)}, u32[]{:S(2)}) collective-permute-start(f32[80,128]{1,0:T(8,128)S(1)} %get-tuple-element.14), channel_id=1, source_target_pairs={{0,1},{1,2},{2,3},{3,4},{4,5},{5,6},{6,7},{7,8},{8,9},{9,10},{10,1... | collective-permute-start | bytes 122888 | tf_op jit(solution)/shard_map/ppermute | solution.py:540
  11.4 1.3 %collective-permute-start.3 = (f32[80,128]{1,0:T(8,128)S(1)}, f32[80,128]{1,0:T(8,128)S(1)}, u32[]{:S(2)}, u32[]{:S(2)}) collective-permute-start(f32[80,128]{1,0:T(8,128)S(1)} %get-tuple-element.15), channel_id=1, source_target_pairs={{1,0},{2,1},{3,2},{4,3},{5,4},{6,5},{7,6},{8,7},{9,8},{10,9},{11,1... | collective-permute-start | bytes 122888 | tf_op jit(solution)/shard_map/ppermute | solution.py:540
  12.7 1.3 %collective-permute-start.1 = (f32[96,128]{1,0:T(8,128)S(1)}, f32[96,128]{1,0:T(8,128)S(1)}, u32[]{:S(2)}, u32[]{:S(2)}) collective-permute-start(f32[96,128]{1,0:T(8,128)S(1)} %get-tuple-element.12.own_left), channel_id=1, source_target_pairs={{16,0},{32,16},{48,32},{64,48},{80,64},{96,80},{112,96},{17,1},{33... | collective-permute-start | bytes 147464 | tf_op jit(solution)/shard_map/ppermute | solution.py:540
  14.0 0.0 copy-start.1
  14.0 0.0 copy-start.3
  14.0 0.0 copy-start.5
  14.0 0.0 copy-start.6
  14.0 0.0 copy-start.7
  14.1 3.3 %collective-permute-start = (f32[96,128]{1,0:T(8,128)S(1)}, f32[96,128]{1,0:T(8,128)S(1)}, u32[]{:S(2)}, u32[]{:S(2)}) collective-permute-start(f32[96,128]{1,0:T(8,128)S(1)} %get-tuple-element.13.own_right), channel_id=1, source_target_pairs={{0,16},{16,32},{32,48},{48,64},{64,80},{80,96},{96,112},{1,17},{17... | collective-permute-start | bytes 147464 | tf_op jit(solution)/shard_map/ppermute | solution.py:540
  17.4 0.0 copy-done.8
  17.4 0.0 copy-done.9
  17.4 0.0 copy-done.10
  17.4 0.0 copy-done.11
  17.4 0.0 copy-done.12
  17.4 0.0 copy-done.13
  17.4 0.0 copy-done.14
  17.4 5.4 %binning.1 = (f32[384,128]{1,0:T(8,128)S(1)}, f32[768,128]{1,0:T(8,128)S(1)}) custom-call(s32[64]{0:T(128)S(1)} %copy-done.14, f32[2,2]{1,0:T(2,128)S(1)} %copy-done.13, f32[64,512]{1,0:T(8,128)S(1)} %copy-done.9, f32[3,64,512]{2,1,0:T(8,128)S(1)} %copy-done.8, f32[64,512]{1,0:T(8,128)S(1)} %copy-done.10, s32[64,512]{1,0:T(8,128)S(1)} %copy-done.11, ...), custom_call_target="tpu_custom_call" | custom-call | flops 4000000000 | bytes 12000000 | tf_op jit(solution)/shard_map/binning/pallas_call | solution.py:171
  22.9 0.0 collective-permute-done.2.from_low
  22.9 0.0 collective-permute-done.3.from_high
  22.9 0.0 collective-permute-done.1.from_right
  22.9 0.0 collective-permute-done.from_left
  22.9 0.0 copy-done.1
  22.9 0.0 copy-done.3
  22.9 0.0 copy-done.5
  22.9 0.0 copy-done.6
  22.9 0.0 copy-done.7
  23.0 24.7 %advect.1 = (f32[5,16,96,128]{3,2,1,0:T(8,128)S(1)}, f32[3072,128]{1,0:T(8,128)S(1)}) custom-call(s32[1,256]{1,0:T(1,128)S(1)} %copy-done.6, s32[64]{0:T(128)S(1)} %copy-done.7, f32[16,96,128]{2,1,0:T(8,128)S(1)} %copy-done.3, f32[3,16,96,128]{3,2,1,0:T(8,128)S(1)} %copy-done.1, f32[16,96,128]{2,1,0:T(8,128)S(1)} %copy-done.5, ...), custom_call_target="tpu_custom_call" | custom-call | flops 4000000000 | bytes 12000000 | tf_op jit(solution)/shard_map/advect/pallas_call | solution.py:371
  47.7 37.1 %all_to_all.5 = f32[128,24,128]{2,1,0:T(8,128)S(1)} all-to-all(f32[128,24,128]{2,1,0:T(8,128)S(1)} %bitcast.3), channel_id=1, replica_groups=mesh['gx'=8,'gy'=16] {'gx','gy'}, dimensions={0} | all-to-all | bytes 3145728 | tf_op jit(solution)/shard_map/all_to_all | solution.py:569
  84.7 5.7 %exchange.1 = (f32[5,16,96,128]{3,2,1,0:T(8,128)}, f32[4,128,128]{2,1,0:T(8,128)}) custom-call(s32[1,256]{1,0:T(1,128)S(1)} %copy-done.6, s32[64]{0:T(128)S(1)} %copy-done.7, f32[3072,128]{1,0:T(8,128)S(1)} %bitcast.4, f32[3072,128]{1,0:T(8,128)S(1)} %get-tuple-element.17.sent, f32[5,16,96,128]{3,2,1,0:T(8,128)S(1)} %get-tuple-element.18.advanced, ...), custom_call_target="tpu_custom_call" | custom-call | tf_op jit(solution)/shard_map/exchange/pallas_call | solution.py:504
Async XLA Ops:
  0.6 1.7 %copy-start = (f32[3,16,96,128]{3,2,1,0:T(8,128)S(1)}, f32[3,16,96,128]{3,2,1,0:T(8,128)}, u32[]{:S(2)}) copy-start(f32[3,16,96,128]{3,2,1,0:T(8,128)} %flow.5) | copy-start | bytes 7077892
  2.3 1.1 %copy-start.2 = (f32[16,96,128]{2,1,0:T(8,128)S(1)}, f32[16,96,128]{2,1,0:T(8,128)}, u32[]{:S(2)}) copy-start(f32[16,96,128]{2,1,0:T(8,128)} %rho.3) | copy-start | bytes 2359300
  3.4 1.1 %copy-start.4 = (f32[16,96,128]{2,1,0:T(8,128)S(1)}, f32[16,96,128]{2,1,0:T(8,128)}, u32[]{:S(2)}) copy-start(f32[16,96,128]{2,1,0:T(8,128)} %kelvin.5) | copy-start | bytes 2359300
  4.6 12.8 %copy-start.8 = (f32[3,64,512]{2,1,0:T(8,128)S(1)}, f32[3,64,512]{2,1,0:T(8,128)}, u32[]{:S(2)}) copy-start(f32[3,64,512]{2,1,0:T(8,128)} %flow.4) | copy-start | bytes 1179652
  4.6 12.8 %copy-start.9 = (f32[64,512]{1,0:T(8,128)S(1)}, f32[64,512]{1,0:T(8,128)}, u32[]{:S(2)}) copy-start(f32[64,512]{1,0:T(8,128)} %mass.1) | copy-start | bytes 393220
  4.6 12.8 %copy-start.10 = (f32[64,512]{1,0:T(8,128)S(1)}, f32[64,512]{1,0:T(8,128)}, u32[]{:S(2)}) copy-start(f32[64,512]{1,0:T(8,128)} %kelvin.4) | copy-start | bytes 393220
  4.6 12.8 %copy-start.11 = (s32[64,512]{1,0:T(8,128)S(1)}, s32[64,512]{1,0:T(8,128)}, u32[]{:S(2)}) copy-start(s32[64,512]{1,0:T(8,128)} %cell.1) | copy-start | bytes 393220
  4.6 12.8 %copy-start.12 = (s32[64,512]{1,0:T(8,128)S(1)}, s32[64,512]{1,0:T(8,128)}, u32[]{:S(2)}) copy-start(s32[64,512]{1,0:T(8,128)} %label.1) | copy-start | bytes 393220
  4.6 12.8 %copy-start.13 = (f32[2,2]{1,0:T(2,128)S(1)}, f32[2,2]{1,0:T(2,128)}, u32[]{:S(2)}) copy-start(f32[2,2]{1,0:T(2,128)} %factor.1) | copy-start | bytes 52
  4.6 12.8 %copy-start.14 = (s32[64]{0:T(128)S(1)}, s32[64]{0:T(128)}, u32[]{:S(2)}) copy-start(s32[64]{0:T(128)} %count.1) | copy-start | bytes 772
  7.8 15.0 %collective-permute-start.2 = (f32[80,128]{1,0:T(8,128)S(1)}, f32[80,128]{1,0:T(8,128)S(1)}, u32[]{:S(2)}, u32[]{:S(2)}) collective-permute-start(f32[80,128]{1,0:T(8,128)S(1)} %get-tuple-element.14), channel_id=1, source_target_pairs={{0,1},{1,2},{2,3},{3,4},{4,5},{5,6},{6,7},{7,8},{8,9},{9,10},{10,1... | collective-permute-start | bytes 122888 | tf_op jit(solution)/shard_map/ppermute | solution.py:540
  11.4 11.5 %collective-permute-start.3 = (f32[80,128]{1,0:T(8,128)S(1)}, f32[80,128]{1,0:T(8,128)S(1)}, u32[]{:S(2)}, u32[]{:S(2)}) collective-permute-start(f32[80,128]{1,0:T(8,128)S(1)} %get-tuple-element.15), channel_id=1, source_target_pairs={{1,0},{2,1},{3,2},{4,3},{5,4},{6,5},{7,6},{8,7},{9,8},{10,9},{11,1... | collective-permute-start | bytes 122888 | tf_op jit(solution)/shard_map/ppermute | solution.py:540
  12.7 10.2 %collective-permute-start.1 = (f32[96,128]{1,0:T(8,128)S(1)}, f32[96,128]{1,0:T(8,128)S(1)}, u32[]{:S(2)}, u32[]{:S(2)}) collective-permute-start(f32[96,128]{1,0:T(8,128)S(1)} %get-tuple-element.12.own_left), channel_id=1, source_target_pairs={{16,0},{32,16},{48,32},{64,48},{80,64},{96,80},{112,96},{17,1},{33... | collective-permute-start | bytes 147464 | tf_op jit(solution)/shard_map/ppermute | solution.py:540
  14.0 8.9 %copy-start.1 = (f32[3,16,96,128]{3,2,1,0:T(8,128)S(1)}, f32[3,16,96,128]{3,2,1,0:T(8,128)}, u32[]{:S(2)}) copy-start(f32[3,16,96,128]{3,2,1,0:T(8,128)} %flow.5) | copy-start | bytes 7077892
  14.0 8.9 %copy-start.3 = (f32[16,96,128]{2,1,0:T(8,128)S(1)}, f32[16,96,128]{2,1,0:T(8,128)}, u32[]{:S(2)}) copy-start(f32[16,96,128]{2,1,0:T(8,128)} %rho.3) | copy-start | bytes 2359300
  14.0 8.9 %copy-start.5 = (f32[16,96,128]{2,1,0:T(8,128)S(1)}, f32[16,96,128]{2,1,0:T(8,128)}, u32[]{:S(2)}) copy-start(f32[16,96,128]{2,1,0:T(8,128)} %kelvin.5) | copy-start | bytes 2359300
  14.0 8.9 %copy-start.6 = (s32[1,256]{1,0:T(1,128)S(1)}, s32[1,256]{1,0:T(1,128)}, u32[]{:S(2)}) copy-start(s32[1,256]{1,0:T(1,128)} %tiles.3) | copy-start | bytes 3076
  14.0 8.9 %copy-start.7 = (s32[64]{0:T(128)S(1)}, s32[64]{0:T(128)}, u32[]{:S(2)}) copy-start(s32[64]{0:T(128)} %rank.3) | copy-start | bytes 772
  14.1 8.8 %collective-permute-start = (f32[96,128]{1,0:T(8,128)S(1)}, f32[96,128]{1,0:T(8,128)S(1)}, u32[]{:S(2)}, u32[]{:S(2)}) collective-permute-start(f32[96,128]{1,0:T(8,128)S(1)} %get-tuple-element.13.own_right), channel_id=1, source_target_pairs={{0,16},{16,32},{32,48},{48,64},{64,80},{80,96},{96,112},{1,17},{17... | collective-permute-start | bytes 147464 | tf_op jit(solution)/shard_map/ppermute | solution.py:540
where the time goes:
time: 90.9 us; the launch traced here: 90.5 us
  Pallas kernels  39.1 us (43%)
  blocking collectives  37.1 us (41%)
  starting transfers between devices  9.45 us (10%)
  local copies, waits for them, and re-layouts  3.98 us (4%)
    all_to_all x1, blocking collectives, per_device(): lax.all_to_all(send.reshape(devices, -1, width), ('gx', 'gy'), split_axis...  37.1 us
    pallas_call x1, Pallas kernels, advect(): pl.pallas_call(advect_kernel, out_shape=(struct(fields, depth, height, wi...  24.7 us
    ppermute x4, starting transfers between devices, shifted(): return lax.ppermute(array, axis, pairs)  9.45 us
    pallas_call x1, Pallas kernels, exchange(): pl.pallas_call(exchange_kernel, out_shape=(struct(*advanced.shape), struc...  5.74 us
    pallas_call x1, Pallas kernels, binning(): pl.pallas_call(binning_kernel, out_shape=(struct(6 * slots, lanes), struc...  5.42 us
    unnamed x30, local copies, waits for them, and re-layouts  3.98 us
    pallas_call x1, Pallas kernels, edges(): pl.pallas_call(edges_kernel, out_shape=(struct(height, width), struct(hei...  3.21 us
  transfers between devices with their start and end apart: 4, of which 0 were waited for; matrix products, arithmetic and copies ran while one was open for 0% of the time, Pallas kernels for 6%

commit v1 on v0

--- a/solution.py
+++ b/solution.py
@@ -10,7 +10,7 @@
 fields = 5
 lanes = 128
 row_pad = 8
-block_rows = 12
+block_rows = 11
 gas_row = 6
 row_chunk = 16
 
@@ -18,6 +18,7 @@
 vmem_spec = pl.BlockSpec(memory_space=pltpu.VMEM)
 smem_spec = pl.BlockSpec(memory_space=pltpu.SMEM)
 any_spec = pl.BlockSpec(memory_space=pl.ANY)
+hbm_spec = pl.BlockSpec(memory_space=pltpu.HBM)
 
 
 def params(mib):
@@ -26,6 +27,14 @@
 
 def struct(*shape):
     return jax.ShapeDtypeStruct(shape, jnp.float32)
+
+
+def near(*shape):
+    return pltpu.VMEM(shape, jnp.float32)
+
+
+def in_hbm(*arrays):
+    return [pltpu.with_memory_space_constraint(a, pltpu.HBM) for a in arrays]
 
 
 def lane_index(shape):
@@ -39,10 +48,11 @@
 
     def copies(part):
         span = pl.ds(part * rows, rows)
+        into = pl.ds(row_pad + part * rows, rows)
         return [
-            pltpu.make_async_copy(rho.at[:, span], held.at[0, :, span], sems.at[0, part]),
-            pltpu.make_async_copy(flow.at[:, :, span], held.at[1:4, :, span], sems.at[1, part]),
-            pltpu.make_async_copy(kelvin.at[:, span], held.at[4, :, span], sems.at[2, part]),
+            pltpu.make_async_copy(rho.at[:, span], held.at[0, :, into], sems.at[0, part]),
+            pltpu.make_async_copy(flow.at[:, :, span], held.at[1:4, :, into], sems.at[1, part]),
+            pltpu.make_async_copy(kelvin.at[:, span], held.at[4, :, into], sems.at[2, part]),
         ]
 
     for part in range(parts):
@@ -56,12 +66,13 @@
         def group(g, carry):
             start = pl.multiple_of(part * rows + g * 8, 8)
             span = pl.ds(start, 8)
+            inside = pl.ds(row_pad + start, 8)
             first = jnp.zeros((8, lanes), jnp.float32)
             last = jnp.zeros((8, lanes), jnp.float32)
             for f in range(fields):
                 for z in range(depth):
                     k = f * depth + z
-                    turned = pltpu.roll(held[f, z, span, :], k + 1, 1)
+                    turned = pltpu.roll(held[f, z, inside, :], k + 1, 1)
                     last = jnp.where(lane == k, turned, last)
                     first = jnp.where(lane == k + 1, turned, first)
             left[span, :] = pltpu.roll(first, lanes - 1, 1)
@@ -72,8 +83,8 @@
     for f in range(fields):
         for z in range(depth):
             k = f * depth + z
-            low[k : k + 1, :] = held[f, z, 0:1, :]
-            high[k : k + 1, :] = held[f, z, height - 1 : height, :]
+            low[k : k + 1, :] = held[f, z, row_pad : row_pad + 1, :]
+            high[k : k + 1, :] = held[f, z, row_pad + height - 1 : row_pad + height, :]
 
 
 def edges(rho, flow, kelvin):
@@ -86,16 +97,16 @@
             struct(height, width),
             struct(fields * depth, width),
             struct(fields * depth, width),
+            near(fields, depth, height + 2 * row_pad, width),
         ),
-        in_specs=[any_spec] * 3,
-        out_specs=(vmem_spec,) * 4,
+        in_specs=[hbm_spec] * 3,
+        out_specs=(vmem_spec,) * 5,
         scratch_shapes=[
-            VM((fields, depth, height, width), jnp.float32),
             pltpu.SemaphoreType.DMA((3, parts)),
         ],
-        compiler_params=params(24),
+        compiler_params=params(16),
         name="edges",
-    )(rho, flow, kelvin)
+    )(*in_hbm(rho, flow, kelvin))
 
 
 def binning_kernel(count, factor, mass, flow, kelvin, cell, label, shared, solid, held, sums):
@@ -197,9 +208,170 @@
     return [through] + [through * c for c in chosen[1:]]
 
 
-def advect_kernel(
+def quotient(a, b, bound):
+    factor = -(-65536 // b)
+    assert all(n * factor // 65536 == n // b for n in range(bound))
+    return (a * factor) // 65536
+
+
+def occupied_kernel(
     tiles,
     rank,
+    state,
+    from_left,
+    from_right,
+    from_low,
+    from_high,
+    shared,
+    send,
+    kept,
+    grab,
+    edge,
+):
+    total = tiles.shape[1]
+    slots = rank.shape[0]
+    depth = state.shape[1]
+    height = state.shape[2] - 2 * row_pad
+    gx, gy = lax.axis_index("gx"), lax.axis_index("gy")
+
+    def keep(wall):
+        return jnp.where(wall, 0.0, 1.0).astype(jnp.float32)
+
+    keep_left = keep(gx == 0)
+    keep_right = keep(gx == lax.axis_size("gx") - 1)
+    keep_low = keep(gy == 0)
+    keep_high = keep(gy == lax.axis_size("gy") - 1)
+    layer = lax.broadcasted_iota(jnp.int32, (8, lanes), 0)
+
+    def gather(i, carry):
+        block = jnp.maximum(tiles[0, i], 0)
+        z = quotient(block, height, depth * height)
+        y = block - z * height
+        lower, upper = jnp.maximum(z - 1, 0), jnp.minimum(z + 1, depth - 1)
+        at_low = layer == jnp.where(y == 0, 0, -1)
+        at_high = layer == jnp.where(y == height - 1, 2, -1)
+        for f in range(fields):
+            k = f * depth + z
+            tile = jnp.where(
+                layer < 3,
+                state[f, z, pl.ds(y + row_pad - 1, 8), :],
+                jnp.where(
+                    layer == 3,
+                    state[f, lower, pl.ds(y + row_pad - 3, 8), :],
+                    state[f, upper, pl.ds(y + row_pad - 4, 8), :],
+                ),
+            )
+            tile = jnp.where(at_low, from_low[pl.ds(k, 1), :], tile)
+            tile = jnp.where(at_high, from_high[pl.ds(k, 1), :], tile)
+            if f == 0:
+                tile = jnp.where(layer == 5, from_left[pl.ds(y, 1), :], tile)
+                tile = jnp.where(layer == 6, from_right[pl.ds(y, 1), :], tile)
+                tile = jnp.where(layer == 7, z.astype(jnp.float32), tile)
+            if f == 1:
+                tile = jnp.where(layer == 7, y.astype(jnp.float32), tile)
+            grab[f, pl.ds(pl.multiple_of(i * 8, 8), 8), :] = tile
+        return carry
+
+    lax.fori_loop(0, total, gather, 0, unroll=4)
+
+    source = lax.broadcasted_iota(jnp.int32, (2 * lanes, fields * lanes), 0)
+    target = lane_index((2 * lanes, fields * lanes))
+    wanted = jnp.where(
+        source < lanes, source // depth * lanes, (source - lanes) // depth * lanes + lanes - 1
+    )
+    chooser = jnp.where(target == wanted, 1.0, 0.0).astype(jnp.bfloat16)
+    level = grab[0, pl.ds(7, total, stride=8), :]
+    lane = lane_index((total, lanes))
+    own = (lane % depth).astype(jnp.float32) == level
+    own = own & (lane < fields * depth)
+    halo = jnp.concatenate(
+        [jnp.where(own, grab[0, pl.ds(5 + c, total, stride=8), :], 0.0) for c in range(2)], 1
+    )
+    coarse = halo.astype(jnp.bfloat16)
+    rest = halo - coarse.astype(jnp.float32)
+    middle = rest.astype(jnp.bfloat16)
+    fine = (rest - middle.astype(jnp.float32)).astype(jnp.bfloat16)
+    edge[...] = (
+        jnp.dot(coarse, chooser, preferred_element_type=jnp.float32)
+        + jnp.dot(middle, chooser, preferred_element_type=jnp.float32)
+        + jnp.dot(fine, chooser, preferred_element_type=jnp.float32)
+    )
+
+    part = 16
+    lane = lane_index((part, lanes))
+    west_keep = jnp.where(lane == 0, keep_left, 1.0)
+    east_keep = jnp.where(lane == lanes - 1, keep_right, 1.0)
+
+    def advance(g, carry):
+        first = pl.multiple_of(g * part, part)
+
+        def rows(f, k):
+            return grab[f, pl.ds(first * 8 + k, part, stride=8), :]
+
+        def states(k):
+            return [rows(f, k) for f in range(fields)]
+
+        z, y = rows(0, 7), rows(1, 7)
+        here = states(1)
+        sides = [
+            edge[pl.ds(first, part), f * lanes : (f + 1) * lanes] for f in range(fields)
+        ]
+        before = [
+            jnp.where(lane == 0, s, pltpu.roll(h, 1, 1)) for s, h in zip(sides, here)
+        ]
+        after = [
+            jnp.where(lane == lanes - 1, s, pltpu.roll(h, lanes - 1, 1))
+            for s, h in zip(sides, here)
+        ]
+        change = [0.0] * fields
+        for a, b, normal, mask, sign in (
+            (states(3), here, 3, jnp.where(z == 0.0, 0.0, 1.0), -1),
+            (here, states(4), 3, jnp.where(z == depth - 1.0, 0.0, 1.0), 1),
+            (states(0), here, 2, jnp.where(y == 0.0, keep_low, 1.0), -1),
+            (here, states(2), 2, jnp.where(y == height - 1.0, keep_high, 1.0), 1),
+            (before, here, 1, west_keep, -1),
+            (here, after, 1, east_keep, 1),
+        ):
+            through = fluxes(a, b, normal, mask)
+            change = [c + t if sign > 0 else c - t for c, t in zip(change, through)]
+        density = here[0] - change[0]
+        inverse = 1.0 / density
+        for f in range(fields):
+            value = density if f == 0 else (here[0] * here[f] - change[f]) * inverse
+            send[pl.ds(first * block_rows + gas_row + f, part, stride=block_rows), :] = value
+            kept[f, pl.ds(first, part), :] = value
+        return carry
+
+    lax.fori_loop(0, total // part, advance, 0)
+
+    def pack_shared(k, carry):
+        slot = jnp.where(rank[k] >= 0, k, 0)
+        row = rank[slot] * block_rows
+        for c in range(6):
+            send[pl.ds(row + c, 1), :] = shared[pl.ds(c * slots + slot, 1), :]
+        return carry
+
+    lax.fori_loop(0, slots, pack_shared, 0, unroll=8)
+
+
+def occupied(tiles, rank, state, received, shared):
+    total = tiles.shape[1]
+    width = state.shape[-1]
+    return pl.pallas_call(
+        occupied_kernel,
+        out_shape=(struct(total * block_rows, width), struct(fields, total, width)),
+        in_specs=[smem_spec] * 2 + [vmem_spec] * 6,
+        out_specs=(vmem_spec,) * 2,
+        scratch_shapes=[
+            VM((fields, total * 8, width), jnp.float32),
+            VM((total, fields * width), jnp.float32),
+        ],
+        compiler_params=params(24),
+        name="occupied",
+    )(tiles, rank, state, *received, shared)
+
+
+def advect_kernel(
     rho,
     flow,
     kelvin,
@@ -209,22 +381,18 @@
     from_right,
     from_low,
     from_high,
-    shared,
     gas_out,
-    send_out,
     state,
     gas,
-    send,
     flux_z,
     flux_y,
     side,
+    side_parts,
+    edge_flux,
     in_sems,
     out_sems,
-    send_sem,
 ):
     depth, height, width = rho.shape
-    cells = depth * height
-    slots = rank.shape[0]
     gx, gy = lax.axis_index("gx"), lax.axis_index("gy")
 
     def keep(wall):
@@ -254,23 +422,38 @@
 
     lax.fori_loop(0, depth, start_loads, 0)
 
+    narrow = lane_index((8, lanes))
+    keep_sides = jnp.where(narrow < depth, keep_left, keep_right)
+
     def boundary(g, carry):
         span = pl.ds(pl.multiple_of(g * 8, 8), 8)
 
-        def split(ref):
-            packed = ref[span, :]
-            return [packed] + [
-                pltpu.roll(packed, lanes - f * depth, 1) for f in range(1, fields)
-            ]
-
-        lower = fluxes(split(from_left), split(own_left), 1, keep_left)
-        upper = fluxes(split(own_right), split(from_right), 1, keep_right)
+        def split(left_faces, right_faces):
+            at_left, at_right = left_faces[span, :], right_faces[span, :]
+            parts = []
+            for f in range(fields):
+                one = pltpu.roll(at_left, (lanes - f * depth) % lanes, 1)
+                two = pltpu.roll(at_right, (lanes + depth - f * depth) % lanes, 1)
+                parts.append(jnp.where(narrow < depth, one, two))
+            return parts
+
+        through = fluxes(split(from_left, own_right), split(own_left, from_right), 1, keep_sides)
         for f in range(fields):
-            side[f, span, :] = lower[f]
-            side[fields + f, span, :] = upper[f]
+            whole = jnp.where(narrow < 2 * depth, through[f], 0.0)
+            coarse = whole.astype(jnp.bfloat16).astype(jnp.float32)
+            rest = whole - coarse
+            middle = rest.astype(jnp.bfloat16).astype(jnp.float32)
+            rest = rest - middle
+            packed = coarse + pltpu.roll(middle, 2 * depth, 1) + pltpu.roll(rest, 4 * depth, 1)
+            side[pl.ds(pl.multiple_of(f * height + g * 8, 8), 8), :] = packed
         return carry
 
     lax.fori_loop(0, height // 8, boundary, 0)
+    side_parts[...] = side[...].astype(jnp.bfloat16)
+    part_row = lax.broadcasted_iota(jnp.int32, (lanes, lanes), 0)
+    place_row = jnp.where(part_row < 6 * depth, part_row % (2 * depth), -1)
+    place_lane = lane_index((lanes, lanes))
+    place_row = jnp.where(place_lane == 0, place_row, jnp.where(place_lane == lanes - 1, place_row - depth, -1))
 
     for f in range(fields):
         flux_z[f] = jnp.zeros((height, width), jnp.float32)
@@ -287,6 +470,8 @@
                 copy.wait()
 
         keep_z = keep(z + 1 == depth)
+        place = jnp.where(place_row == z, 1.0, 0.0).astype(jnp.bfloat16)
+        edge_flux[...] = jnp.dot(side_parts[...], place, preferred_element_type=jnp.float32)
         for f in range(fields):
             k = f * depth + z
             state[f, z, row_pad - 1 : row_pad, :] = from_low[pl.ds(k, 1), :]
@@ -320,10 +505,9 @@
             before = [pltpu.roll(h, 1, 1) for h in here]
             faces = fluxes(before, here, 1)
             for f in range(fields):
-                lower = pltpu.roll(side[f, span, :], lanes - z, 1)
-                upper = pltpu.roll(side[fields + f, span, :], lanes - 1 - z, 1)
-                face = jnp.where(lane == 0, lower, faces[f])
-                after = jnp.where(lane == lanes - 1, upper, pltpu.roll(face, lanes - 1, 1))
+                edge = edge_flux[pl.ds(f * height + start, row_chunk), :]
+                face = jnp.where(lane == 0, edge, faces[f])
+                after = jnp.where(lane == lanes - 1, edge, pltpu.roll(face, lanes - 1, 1))
                 change[f] = change[f] + (after - face)
             density = here[0] - change[0]
             inverse = 1.0 / density
@@ -336,63 +520,37 @@
 
     lax.fori_loop(0, depth, plane, 0)
 
-    total = tiles.shape[1]
-
-    def pack_gas(i, carry):
-        block = jnp.maximum(tiles[0, i], 0)
-        for f in range(fields):
-            send[pl.ds(i * block_rows + gas_row + f, 1), :] = gas[f, pl.ds(block, 1), :]
-        return carry
-
-    lax.fori_loop(0, total, pack_gas, 0, unroll=8)
-
-    def pack_shared(k, carry):
-        where_to = rank[k]
-        row = jnp.where(where_to >= 0, where_to, total) * block_rows
-        for c in range(6):
-            send[pl.ds(row + c, 1), :] = shared[pl.ds(c * slots + k, 1), :]
-        return carry
-
-    lax.fori_loop(0, slots, pack_shared, 0, unroll=4)
-    copy = pltpu.make_async_copy(send.at[pl.ds(0, total * block_rows)], send_out, send_sem)
-    copy.start()
-
     def finish(z, carry):
         store(z).wait()
         return carry
 
     lax.fori_loop(0, depth, finish, 0)
-    copy.wait()
-
-
-def advect(tiles, rank, rho, flow, kelvin, own, received, shared):
+
+
+def advect(rho, flow, kelvin, own, received):
     depth, height, width = rho.shape
-    total = tiles.shape[1]
     return pl.pallas_call(
         advect_kernel,
-        out_shape=(
-            struct(fields, depth, height, width),
-            struct(total * block_rows, width),
-        ),
-        in_specs=[smem_spec] * 2 + [any_spec] * 3 + [vmem_spec] * 7,
-        out_specs=(any_spec,) * 2,
+        out_shape=pltpu.HBM((fields, depth, height, width), jnp.float32),
+        in_specs=[hbm_spec] * 3 + [vmem_spec] * 6,
+        out_specs=hbm_spec,
         scratch_shapes=[
             VM((fields, depth, height + 2 * row_pad, width), jnp.float32),
             VM((fields, depth * height, width), jnp.float32),
-            VM(((total + 2) * block_rows, width), jnp.float32),
             VM((fields, height, width), jnp.float32),
             VM((fields, height + row_pad, width), jnp.float32),
-            VM((2 * fields, height, width), jnp.float32),
+            VM((fields * height, width), jnp.float32),
+            VM((fields * height, width), jnp.bfloat16),
+            VM((fields * height, width), jnp.float32),
             pltpu.SemaphoreType.DMA((3, depth)),
             pltpu.SemaphoreType.DMA((depth,)),
-            pltpu.SemaphoreType.DMA,
         ],
         cost_estimate=pl.CostEstimate(
             flops=4_000_000_000, bytes_accessed=12_000_000, transcendentals=0
         ),
-        compiler_params=params(32),
+        compiler_params=params(24),
         name="advect",
-    )(tiles, rank, rho, flow, kelvin, *own, *received, shared)
+    )(*in_hbm(rho, flow, kelvin), *own, *received)
 
 
 def mixed(density, gas, sums):
@@ -406,7 +564,7 @@
     tiles,
     rank,
     received,
-    sent,
+    kept,
     advanced,
     shared,
     solid,
@@ -418,23 +576,52 @@
     in_sems,
     out_sems,
 ):
-    _, depth, height, width = advanced.shape
+    _, depth, height, width = gas_out.shape
     cells = depth * height
     total = tiles.shape[1]
     slots = rank.shape[0]
-
-    def load(f):
+    part = 32
+
+    def load(c):
         return pltpu.make_async_copy(
-            advanced.at[f], gas.at[f, pl.ds(0, depth)], in_sems.at[f]
+            advanced.at[1 + c], gas.at[c, pl.ds(0, depth)], in_sems.at[c]
         )
 
-    for f in range(fields):
-        load(f).start()
-
-    def store(f):
+    def store(c):
         return pltpu.make_async_copy(
-            gas.at[f, pl.ds(0, depth)], gas_out.at[f], out_sems.at[f]
+            gas.at[c, pl.ds(0, depth)], gas_out.at[1 + c], out_sems.at[c]
         )
+
+    for c in range(4):
+        load(c).start()
+
+    def blocks(g, carry):
+        first = pl.multiple_of(g * part, part)
+        span = pl.ds(first, part)
+        result = mixed(
+            kept[0, span, :],
+            [kept[1 + c, span, :] for c in range(4)],
+            [received[pl.ds(first * block_rows + c, part, stride=block_rows), :] for c in range(6)],
+        )
+        for c in range(4):
+            fresh[c, span, :] = result[c]
+        return carry
+
+    lax.fori_loop(0, total // part, blocks, 0)
+    for c in range(4):
+        load(c).wait()
+
+    def scatter(i, carry):
+        block = tiles[0, i]
+        block = jnp.where(block >= 0, block, cells)
+        z = quotient(block, height, cells + 1)
+        for c in range(4):
+            gas[c, z, pl.ds(block - z * height, 1), :] = fresh[c, pl.ds(i, 1), :]
+        return carry
+
+    lax.fori_loop(0, total, scatter, 0, unroll=8)
+    for c in range(4):
+        store(c).start()
 
     def gather(k, live):
         spot = rank[k]
@@ -444,42 +631,6 @@
         return live + jnp.where(spot >= 0, 1, 0)
 
     live = lax.fori_loop(0, slots, gather, 0, unroll=4)
-
-    part = 32
-
-    def blocks(g, carry):
-        first = pl.multiple_of(g * part, part)
-
-        def rows(ref, c):
-            return ref[pl.ds(first * block_rows + c, part, stride=block_rows), :]
-
-        result = mixed(
-            rows(sent, gas_row),
-            [rows(sent, gas_row + 1 + c) for c in range(4)],
-            [rows(received, c) for c in range(6)],
-        )
-        for c in range(4):
-            fresh[c, pl.ds(first, part), :] = result[c]
-        return carry
-
-    lax.fori_loop(0, total // part, blocks, 0)
-    for f in range(fields):
-        load(f).wait()
-    store(0).start()
-
-    def scatter(i, carry):
-        block = tiles[0, i]
-        block = jnp.where(block >= 0, block, cells)
-        z = block // height
-        y = block - z * height
-        for c in range(4):
-            gas[1 + c, z, pl.ds(y, 1), :] = fresh[c, pl.ds(i, 1), :]
-        return carry
-
-    lax.fori_loop(0, total, scatter, 0, unroll=8)
-    for f in range(1, fields):
-        store(f).start()
-
     result = mixed(
         slot_gas[0],
         [slot_gas[1 + c] for c in range(4)],
@@ -493,29 +644,30 @@
             solid_out[c, pl.ds(m, slots, stride=2), :] = jnp.where(
                 alive, base + scale * result[c], 0.0
             )
-    for f in range(fields):
-        store(f).wait()
-
-
-def exchange(tiles, rank, received, sent, advanced, shared, solid):
+    for c in range(4):
+        store(c).wait()
+
+
+def exchange(tiles, rank, received, kept, advanced, shared, solid):
     _, depth, height, width = advanced.shape
     total = tiles.shape[1]
     slots = rank.shape[0]
     return pl.pallas_call(
         exchange_kernel,
-        out_shape=(struct(*advanced.shape), struct(4, 2 * slots, width)),
-        in_specs=[smem_spec] * 2 + [vmem_spec] * 2 + [any_spec] + [vmem_spec] * 2,
-        out_specs=(any_spec, vmem_spec),
+        out_shape=(pltpu.HBM(advanced.shape, jnp.float32), struct(4, 2 * slots, width)),
+        in_specs=[smem_spec] * 2 + [vmem_spec] * 2 + [hbm_spec] + [vmem_spec] * 2,
+        out_specs=(hbm_spec, vmem_spec),
         scratch_shapes=[
-            VM((fields, depth + 1, height, width), jnp.float32),
+            VM((4, depth + 1, height, width), jnp.float32),
             VM((4, total, width), jnp.float32),
             VM((fields, slots, width), jnp.float32),
-            pltpu.SemaphoreType.DMA((fields,)),
-            pltpu.SemaphoreType.DMA((fields,)),
+            pltpu.SemaphoreType.DMA((4,)),
+            pltpu.SemaphoreType.DMA((4,)),
         ],
-        compiler_params=params(32),
+        input_output_aliases={4: 0},
+        compiler_params=params(24),
         name="exchange",
-    )(tiles, rank, received, sent, advanced, shared, solid)
+    )(tiles, rank, received, kept, *in_hbm(advanced), shared, solid)
 
 
 def per_device(
@@ -532,12 +684,11 @@
     grain_substance_label,
     exchange_factor,
 ):
-    left, right, low, high = edges(gaseous_rho, gaseous_flow_vector, gaseous_kelvin)
+    left, right, low, high, state = edges(gaseous_rho, gaseous_flow_vector, gaseous_kelvin)
 
     def shifted(array, axis, step):
         count = lax.axis_size(axis)
-        pairs = [(i, i + step) for i in range(count) if 0 <= i + step < count]
-        return lax.ppermute(array, axis, pairs)
+        return lax.ppermute(array, axis, [(i, (i + step) % count) for i in range(count)])
 
     received = (
         shifted(right, "gx", 1),
@@ -554,26 +705,20 @@
         grain_voxel_number,
         grain_substance_label,
     )
-    advanced, send = advect(
-        sender_tile_map,
-        receiver_arrival_rank,
-        gaseous_rho,
-        gaseous_flow_vector,
-        gaseous_kelvin,
-        (left, right),
-        received,
-        shared,
-    )
+    send, kept = occupied(sender_tile_map, receiver_arrival_rank, state, received, shared)
     devices = lax.axis_size("gx") * lax.axis_size("gy")
     width = send.shape[-1]
     arrived = lax.all_to_all(
-        send.reshape(devices, -1, width), ("gx", "gy"), split_axis=0, concat_axis=0, tiled=True
+        send.reshape(devices, block_rows, -1, width), ("gx", "gy"), split_axis=0, concat_axis=0, tiled=True
+    )
+    advanced = advect(
+        gaseous_rho, gaseous_flow_vector, gaseous_kelvin, (left, right), received
     )
     gas_state, solid_state = exchange(
         sender_tile_map,
         receiver_arrival_rank,
         arrived.reshape(-1, width),
-        send,
+        kept,
         advanced,
         shared,
         solid,

time: 90.9 us -> 63.9 us (0.70)
  blocking collectives: 37.1 us -> 0 us
  waiting for transfers between devices: 0.01 us -> 13.3 us
  starting transfers between devices: 9.45 us -> 15 us
  Pallas kernels: 39.1 us -> 34.5 us
  local copies, waits for them, and re-layouts: 3.98 us -> 0.04 us
    all_to_all x1 -> x0, blocking collectives: 37.1 us -> none  [per_device(): lax.all_to_all(send.reshape(devices, -1, width), ('gx', 'gy'), split_axis...]
    all_to_all x0 -> x1, waiting for transfers between devices: none -> 13.3 us  [per_device(): lax.all_to_all(send.reshape(devices, block_rows, -1, width), ('gx', 'gy')...]
    all_to_all x0 -> x1, starting transfers between devices: none -> 6.34 us  [per_device(): lax.all_to_all(send.reshape(devices, block_rows, -1, width), ('gx', 'gy')...]
    pallas_call x2 -> x3, Pallas kernels: 30.5 us -> 25 us  [the longest x1 9.78 us: advect(): pl.pallas_call(advect_kernel, out_shape=pltpu.HBM((fields, depth, height,...]
    unnamed x30 -> x18, local copies, waits for them, and re-layouts: 3.98 us -> 0.04 us
  transfers between devices with their start and end apart: 4 -> 5, of which waited for: 0 -> 1; matrix products, arithmetic and copies ran while one was open for 0% -> 0% of each run, Pallas kernels for 6% -> 24%
where the time goes in v1:
time: 63.9 us; the launch traced here: 63.7 us
  Pallas kernels  34.5 us (54%)
  starting transfers between devices  15 us (23%)
  waiting for transfers between devices  13.3 us (21%)
  between operations  0.8 us (1%)
    all_to_all x1, waiting for transfers between devices, per_device(): lax.all_to_all(send.reshape(devices, block_rows, -1, width), ('gx', 'gy')...  13.3 us
    pallas_call x1, Pallas kernels, advect(): pl.pallas_call(advect_kernel, out_shape=pltpu.HBM((fields, depth, height,...  9.78 us
    ppermute x4, starting transfers between devices, shifted(): lax.ppermute(array, axis, [(i, (i + step) % count) for i in range(count)])  8.64 us
    pallas_call x1, Pallas kernels, occupied(): pl.pallas_call(occupied_kernel, out_shape=(struct(total * block_rows, wid...  8.53 us
    pallas_call x1, Pallas kernels, exchange(): pl.pallas_call(exchange_kernel, out_shape=(pltpu.HBM(advanced.shape, jnp....  6.73 us
    all_to_all x1, starting transfers between devices, per_device(): lax.all_to_all(send.reshape(devices, block_rows, -1, width), ('gx', 'gy')...  6.34 us
    pallas_call x1, Pallas kernels, binning(): pl.pallas_call(binning_kernel, out_shape=(struct(6 * slots, lanes), struc...  5.42 us
    pallas_call x1, Pallas kernels, edges(): pl.pallas_call(edges_kernel, out_shape=(struct(height, width), struct(hei...  4.06 us
  transfers between devices with their start and end apart: 5, of which 1 were waited for; matrix products, arithmetic and copies ran while one was open for 0% of the time, Pallas kernels for 24%

profile of v1, /device:TPU:0, one launch (start us, length us, event | category | flops | bytes accessed | tf_op | source)
XLA Modules:
  0.0 63.7 jit_solution(7714695942419343966)
XLA Ops:
  0.6 0.0 copy-start.7
  0.6 0.0 copy-start.6
  0.7 0.0 copy-start.5
  0.7 0.0 copy-start.4
  0.7 0.0 copy-start.2
  0.7 0.0 copy-start.3
  0.7 0.0 copy-start.8
  0.7 4.1 %edges.1 = (f32[96,128]{1,0:T(8,128)S(1)}, f32[96,128]{1,0:T(8,128)S(1)}, f32[80,128]{1,0:T(8,128)S(1)}, f32[80,128]{1,0:T(8,128)S(1)}, f32[5,16,112,128]{3,2,1,0:T(8,128)S(1)}) custom-call(f32[16,96,128]{2,1,0:T(8,128)} %rho.3, f32[3,16,96,128]{3,2,1,0:T(8,128)} %flow.5, f32[16,96,128]{2,1,0:T(8,128)} %kelvin.5), custom_call_target="tpu_custom_call" | custom-call | tf_op jit(solution)/shard_map/edges/pallas_call | solution.py:93
  4.8 1.7 %collective-permute-start.2 = (f32[80,128]{1,0:T(8,128)S(1)}, f32[80,128]{1,0:T(8,128)S(1)}, u32[]{:S(2)}, u32[]{:S(2)}) collective-permute-start(f32[80,128]{1,0:T(8,128)S(1)} %get-tuple-element.16), channel_id=1, source_target_pairs={{0,1},{1,2},{2,3},{3,4},{4,5},{5,6},{6,7},{7,8},{8,9},{9,10},{10,1... | collective-permute-start | bytes 122888 | tf_op jit(solution)/shard_map/ppermute | solution.py:691
  6.5 3.7 %collective-permute-start.3 = (f32[80,128]{1,0:T(8,128)S(1)}, f32[80,128]{1,0:T(8,128)S(1)}, u32[]{:S(2)}, u32[]{:S(2)}) collective-permute-start(f32[80,128]{1,0:T(8,128)S(1)} %get-tuple-element.17), channel_id=1, source_target_pairs={{0,15},{1,0},{2,1},{3,2},{4,3},{5,4},{6,5},{7,6},{8,7},{9,8},{10,9... | collective-permute-start | bytes 122888 | tf_op jit(solution)/shard_map/ppermute | solution.py:691
  10.2 0.0 collective-permute-start
  10.2 0.0 copy-start
  10.2 0.0 copy-start.1
  10.2 3.2 %collective-permute-start.1 = (f32[96,128]{1,0:T(8,128)S(1)}, f32[96,128]{1,0:T(8,128)S(1)}, u32[]{:S(2)}, u32[]{:S(2)}) collective-permute-start(f32[96,128]{1,0:T(8,128)S(1)} %get-tuple-element.15.own_left), channel_id=1, source_target_pairs={{0,112},{16,0},{32,16},{48,32},{64,48},{80,64},{96,80},{112,96},{1... | collective-permute-start | bytes 147464 | tf_op jit(solution)/shard_map/ppermute | solution.py:691
  13.4 0.0 copy-done.7
  13.4 0.0 copy-done.6
  13.4 0.0 copy-done.5
  13.4 0.0 copy-done.4
  13.4 0.0 copy-done.2
  13.4 0.0 copy-done.3
  13.5 0.0 copy-done.8
  13.5 5.4 %binning.1 = (f32[384,128]{1,0:T(8,128)S(1)}, f32[768,128]{1,0:T(8,128)S(1)}) custom-call(s32[64]{0:T(128)S(1)} %copy-done.8, f32[2,2]{1,0:T(2,128)S(1)} %copy-done.7, f32[64,512]{1,0:T(8,128)S(1)} %copy-done.3, f32[3,64,512]{2,1,0:T(8,128)S(1)} %copy-done.2, f32[64,512]{1,0:T(8,128)S(1)} %copy-done.4, s32[64,512]{1,0:T(8,128)S(1)} %copy-done.5, ...), custom_call_target="tpu_custom_call" | custom-call | flops 4000000000 | bytes 12000000 | tf_op jit(solution)/shard_map/binning/pallas_call | solution.py:182
  18.9 0.0 collective-permute-done.2.from_low
  18.9 0.0 collective-permute-done.3.from_high
  18.9 0.0 collective-permute-done.from_left
  18.9 0.0 collective-permute-done.1.from_right
  18.9 0.0 copy-done
  18.9 0.0 copy-done.1
  19.0 8.5 %occupied.1 = (f32[2816,128]{1,0:T(8,128)}, f32[5,256,128]{2,1,0:T(8,128)S(1)}) custom-call(s32[1,256]{1,0:T(1,128)S(1)} %copy-done, s32[64]{0:T(128)S(1)} %copy-done.1, f32[5,16,112,128]{3,2,1,0:T(8,128)S(1)} %get-tuple-element.13.state, f32[96,128]{1,0:T(8,128)S(1)} %collective-permute-done.from_left, f32[96,128]{1,0:T(8,128)S(1)} %collective-permute-done.1.from_right, ...), custom_call_target="tpu_custom_call" | custom-call | tf_op jit(solution)/shard_map/occupied/pallas_call | solution.py:360
  27.5 6.3 %all-to-all-start = ((f32[128,11,2,128]{3,2,1,0:T(2,128)}), f32[128,11,2,128]{3,2,1,0:T(2,128)S(1)}, u32[]{:S(2)}, u32[]{:S(2)}) async-start(f32[128,11,2,128]{3,2,1,0:T(2,128)} %bitcast), calls=%async_computation | async-start | bytes 2883584 | tf_op jit(solution)/shard_map/all_to_all | solution.py:711
  33.8 9.8 %advect.1.advanced = f32[5,16,96,128]{3,2,1,0:T(8,128)} custom-call(f32[16,96,128]{2,1,0:T(8,128)} %rho.3, f32[3,16,96,128]{3,2,1,0:T(8,128)} %flow.5, f32[16,96,128]{2,1,0:T(8,128)} %kelvin.5, f32[96,128]{1,0:T(8,128)S(1)} %get-tuple-element.15.own_left, f32[96,128]{1,0:T(8,128)S(1)} %get-tuple-element.14.own_right, ...), custom_call_target="tpu_custom_call" | custom-call | flops 4000000000 | bytes 12000000 | tf_op jit(solution)/shard_map/advect/pallas_call | solution.py:532
  43.6 13.3 %all-to-all-done = f32[128,11,2,128]{3,2,1,0:T(2,128)S(1)} async-done(((f32[128,11,2,128]{3,2,1,0:T(2,128)}), f32[128,11,2,128]{3,2,1,0:T(2,128)S(1)}, u32[]{:S(2)}, u32[]{:S(2)}) %all-to-all-start) | async-done | bytes 1441824 | tf_op jit(solution)/shard_map/all_to_all | solution.py:711
  57.0 6.7 %exchange.1 = (f32[5,16,96,128]{3,2,1,0:T(8,128)}, f32[4,128,128]{2,1,0:T(8,128)}) custom-call(s32[1,256]{1,0:T(1,128)S(1)} %copy-done, s32[64]{0:T(128)S(1)} %copy-done.1, f32[2816,128]{1,0:T(8,128)S(1)} %bitcast.3, f32[5,256,128]{2,1,0:T(8,128)S(1)} %get-tuple-element.20.kept, f32[5,16,96,128]{3,2,1,0:T(8,128)} %advect.1.advanced, ...), custom_call_target="tpu_custom_call", output_to_operand_aliasing={{0}: (4, {})} | custom-call | tf_op jit(solution)/shard_map/exchange/pallas_call | solution.py:655
Async XLA Ops:
  0.6 12.8 %copy-start.7 = (f32[2,2]{1,0:T(2,128)S(1)}, f32[2,2]{1,0:T(2,128)}, u32[]{:S(2)}) copy-start(f32[2,2]{1,0:T(2,128)} %factor.1) | copy-start | bytes 52
  0.6 12.8 %copy-start.6 = (s32[64,512]{1,0:T(8,128)S(1)}, s32[64,512]{1,0:T(8,128)}, u32[]{:S(2)}) copy-start(s32[64,512]{1,0:T(8,128)} %label.1) | copy-start | bytes 393220
  0.7 12.8 %copy-start.5 = (s32[64,512]{1,0:T(8,128)S(1)}, s32[64,512]{1,0:T(8,128)}, u32[]{:S(2)}) copy-start(s32[64,512]{1,0:T(8,128)} %cell.1) | copy-start | bytes 393220
  0.7 12.8 %copy-start.4 = (f32[64,512]{1,0:T(8,128)S(1)}, f32[64,512]{1,0:T(8,128)}, u32[]{:S(2)}) copy-start(f32[64,512]{1,0:T(8,128)} %kelvin.4) | copy-start | bytes 393220
  0.7 12.8 %copy-start.2 = (f32[3,64,512]{2,1,0:T(8,128)S(1)}, f32[3,64,512]{2,1,0:T(8,128)}, u32[]{:S(2)}) copy-start(f32[3,64,512]{2,1,0:T(8,128)} %flow.4) | copy-start | bytes 1179652
  0.7 12.8 %copy-start.3 = (f32[64,512]{1,0:T(8,128)S(1)}, f32[64,512]{1,0:T(8,128)}, u32[]{:S(2)}) copy-start(f32[64,512]{1,0:T(8,128)} %mass.1) | copy-start | bytes 393220
  0.7 12.8 %copy-start.8 = (s32[64]{0:T(128)S(1)}, s32[64]{0:T(128)}, u32[]{:S(2)}) copy-start(s32[64]{0:T(128)} %count.1) | copy-start | bytes 772
  4.8 14.1 %collective-permute-start.2 = (f32[80,128]{1,0:T(8,128)S(1)}, f32[80,128]{1,0:T(8,128)S(1)}, u32[]{:S(2)}, u32[]{:S(2)}) collective-permute-start(f32[80,128]{1,0:T(8,128)S(1)} %get-tuple-element.16), channel_id=1, source_target_pairs={{0,1},{1,2},{2,3},{3,4},{4,5},{5,6},{6,7},{7,8},{8,9},{9,10},{10,1... | collective-permute-start | bytes 122888 | tf_op jit(solution)/shard_map/ppermute | solution.py:691
  6.5 12.4 %collective-permute-start.3 = (f32[80,128]{1,0:T(8,128)S(1)}, f32[80,128]{1,0:T(8,128)S(1)}, u32[]{:S(2)}, u32[]{:S(2)}) collective-permute-start(f32[80,128]{1,0:T(8,128)S(1)} %get-tuple-element.17), channel_id=1, source_target_pairs={{0,15},{1,0},{2,1},{3,2},{4,3},{5,4},{6,5},{7,6},{8,7},{9,8},{10,9... | collective-permute-start | bytes 122888 | tf_op jit(solution)/shard_map/ppermute | solution.py:691
  10.2 8.7 %collective-permute-start = (f32[96,128]{1,0:T(8,128)S(1)}, f32[96,128]{1,0:T(8,128)S(1)}, u32[]{:S(2)}, u32[]{:S(2)}) collective-permute-start(f32[96,128]{1,0:T(8,128)S(1)} %get-tuple-element.14.own_right), channel_id=1, source_target_pairs={{0,16},{16,32},{32,48},{48,64},{64,80},{80,96},{96,112},{112,0},{1... | collective-permute-start | bytes 147464 | tf_op jit(solution)/shard_map/ppermute | solution.py:691
  10.2 8.7 %copy-start = (s32[1,256]{1,0:T(1,128)S(1)}, s32[1,256]{1,0:T(1,128)}, u32[]{:S(2)}) copy-start(s32[1,256]{1,0:T(1,128)} %tiles.3) | copy-start | bytes 3076
  10.2 8.7 %copy-start.1 = (s32[64]{0:T(128)S(1)}, s32[64]{0:T(128)}, u32[]{:S(2)}) copy-start(s32[64]{0:T(128)} %rank.3) | copy-start | bytes 772
  10.2 8.7 %collective-permute-start.1 = (f32[96,128]{1,0:T(8,128)S(1)}, f32[96,128]{1,0:T(8,128)S(1)}, u32[]{:S(2)}, u32[]{:S(2)}) collective-permute-start(f32[96,128]{1,0:T(8,128)S(1)} %get-tuple-element.15.own_left), channel_id=1, source_target_pairs={{0,112},{16,0},{32,16},{48,32},{64,48},{80,64},{96,80},{112,96},{1... | collective-permute-start | bytes 147464 | tf_op jit(solution)/shard_map/ppermute | solution.py:691
  27.5 29.5 %all-to-all-start = ((f32[128,11,2,128]{3,2,1,0:T(2,128)}), f32[128,11,2,128]{3,2,1,0:T(2,128)S(1)}, u32[]{:S(2)}, u32[]{:S(2)}) async-start(f32[128,11,2,128]{3,2,1,0:T(2,128)} %bitcast), calls=%async_computation | async-start | bytes 2883584 | tf_op jit(solution)/shard_map/all_to_all | solution.py:711

commit v2 on v1

--- a/solution.py
+++ b/solution.py
@@ -50,41 +50,40 @@
         span = pl.ds(part * rows, rows)
         into = pl.ds(row_pad + part * rows, rows)
         return [
-            pltpu.make_async_copy(rho.at[:, span], held.at[0, :, into], sems.at[0, part]),
-            pltpu.make_async_copy(flow.at[:, :, span], held.at[1:4, :, into], sems.at[1, part]),
-            pltpu.make_async_copy(kelvin.at[:, span], held.at[4, :, into], sems.at[2, part]),
+            pltpu.make_async_copy(rho.at[:, span], held.at[0, pl.ds(1, depth), into], sems.at[0, part]),
+            pltpu.make_async_copy(flow.at[:, :, span], held.at[1:4, pl.ds(1, depth), into], sems.at[1, part]),
+            pltpu.make_async_copy(kelvin.at[:, span], held.at[4, pl.ds(1, depth), into], sems.at[2, part]),
         ]
 
     for part in range(parts):
         for copy in copies(part):
             copy.start()
-    lane = lane_index((8, lanes))
+    lane = lane_index((rows, lanes))
     for part in range(parts):
         for copy in copies(part):
             copy.wait()
 
-        def group(g, carry):
-            start = pl.multiple_of(part * rows + g * 8, 8)
-            span = pl.ds(start, 8)
-            inside = pl.ds(row_pad + start, 8)
-            first = jnp.zeros((8, lanes), jnp.float32)
-            last = jnp.zeros((8, lanes), jnp.float32)
-            for f in range(fields):
-                for z in range(depth):
-                    k = f * depth + z
-                    turned = pltpu.roll(held[f, z, inside, :], k + 1, 1)
-                    last = jnp.where(lane == k, turned, last)
-                    first = jnp.where(lane == k + 1, turned, first)
-            left[span, :] = pltpu.roll(first, lanes - 1, 1)
-            right[span, :] = last
-            return carry
-
-        lax.fori_loop(0, rows // 8, group, 0)
+        span = pl.ds(part * rows, rows)
+        inside = pl.ds(row_pad + part * rows, rows)
+        first = jnp.zeros((rows, lanes), jnp.float32)
+        last = jnp.zeros((rows, lanes), jnp.float32)
+        for f in range(fields):
+            for z in range(depth):
+                k = f * depth + z
+                turned = pltpu.roll(held[f, z + 1, inside, :], k + 1, 1)
+                last = jnp.where(lane == k, turned, last)
+                first = jnp.where(lane == k + 1, turned, first)
+        left[span, :] = pltpu.roll(first, lanes - 1, 1)
+        right[span, :] = last
     for f in range(fields):
         for z in range(depth):
             k = f * depth + z
-            low[k : k + 1, :] = held[f, z, row_pad : row_pad + 1, :]
-            high[k : k + 1, :] = held[f, z, row_pad + height - 1 : row_pad + height, :]
+            low[k : k + 1, :] = held[f, z + 1, row_pad : row_pad + 1, :]
+            high[k : k + 1, :] = held[f, z + 1, row_pad + height - 1 : row_pad + height, :]
+    for f in range(fields):
+        sign = -1.0 if f == 3 else 1.0
+        held[f, 0] = sign * held[f, 1]
+        held[f, depth + 1] = sign * held[f, depth]
 
 
 def edges(rho, flow, kelvin):
@@ -97,7 +96,7 @@
             struct(height, width),
             struct(fields * depth, width),
             struct(fields * depth, width),
-            near(fields, depth, height + 2 * row_pad, width),
+            near(fields, depth + 2, height + 2 * row_pad, width),
         ),
         in_specs=[hbm_spec] * 3,
         out_specs=(vmem_spec,) * 5,
@@ -149,7 +148,7 @@
         sums[pl.ds(pl.multiple_of(s * 16, 16), 16), :] = summed[0:16] + summed[16:32]
         return carry
 
-    lax.fori_loop(0, slots, slot_sums, 0, unroll=4)
+    lax.fori_loop(0, slots, slot_sums, 0, unroll=32)
     totals = [0.0] * 6
     for m in range(2):
         drag, thermal = factor[m, 0], factor[m, 1]
@@ -211,78 +210,91 @@
 def quotient(a, b, bound):
     factor = -(-65536 // b)
     assert all(n * factor // 65536 == n // b for n in range(bound))
-    return (a * factor) // 65536
+    return lax.shift_right_logical(a * factor, 16)
 
 
 def occupied_kernel(
     tiles,
     rank,
-    state,
+    _,
+    own_left,
+    own_right,
     from_left,
     from_right,
     from_low,
     from_high,
     shared,
+    send_out,
+    kept,
+    state,
     send,
-    kept,
     grab,
     edge,
+    west,
+    east,
+    sems,
 ):
     total = tiles.shape[1]
     slots = rank.shape[0]
-    depth = state.shape[1]
-    height = state.shape[2] - 2 * row_pad
+    height = from_left.shape[0]
+    depth = from_low.shape[0] // fields
+    pitch = height + 2 * row_pad
     gx, gy = lax.axis_index("gx"), lax.axis_index("gy")
 
-    def keep(wall):
-        return jnp.where(wall, 0.0, 1.0).astype(jnp.float32)
-
-    keep_left = keep(gx == 0)
-    keep_right = keep(gx == lax.axis_size("gx") - 1)
-    keep_low = keep(gy == 0)
-    keep_high = keep(gy == lax.axis_size("gy") - 1)
+    def walled(wall, f, normal, own, other):
+        return jnp.where(wall, -own if f == normal else own, other)
+
+    for f in range(fields):
+        for z in range(depth):
+            k = slice(f * depth + z, f * depth + z + 1)
+            row = (z + 1) * pitch + row_pad
+            state[f, row - 1 : row, :] = walled(
+                gy == 0, f, 2, state[f, row : row + 1, :], from_low[k, :]
+            )
+            row = row + height - 1
+            state[f, row + 1 : row + 2, :] = walled(
+                gy == lax.axis_size("gy") - 1, f, 2, state[f, row : row + 1, :], from_high[k, :]
+            )
+    lane = lane_index((height, lanes))
+    sign = jnp.where((lane >= depth) & (lane < 2 * depth), -1.0, 1.0)
+    west[...] = jnp.where(gx == 0, sign * own_left[...], from_left[...])
+    east[...] = jnp.where(gx == lax.axis_size("gx") - 1, sign * own_right[...], from_right[...])
+
+    assert depth & (depth - 1) == 0
     layer = lax.broadcasted_iota(jnp.int32, (8, lanes), 0)
 
     def gather(i, carry):
         block = jnp.maximum(tiles[0, i], 0)
         z = quotient(block, height, depth * height)
         y = block - z * height
-        lower, upper = jnp.maximum(z - 1, 0), jnp.minimum(z + 1, depth - 1)
-        at_low = layer == jnp.where(y == 0, 0, -1)
-        at_high = layer == jnp.where(y == height - 1, 2, -1)
+        base = block + z * (pitch - height) + pitch + row_pad
         for f in range(fields):
-            k = f * depth + z
             tile = jnp.where(
                 layer < 3,
-                state[f, z, pl.ds(y + row_pad - 1, 8), :],
+                state[f, pl.ds(base - 1, 8), :],
                 jnp.where(
                     layer == 3,
-                    state[f, lower, pl.ds(y + row_pad - 3, 8), :],
-                    state[f, upper, pl.ds(y + row_pad - 4, 8), :],
+                    state[f, pl.ds(base - pitch - 3, 8), :],
+                    state[f, pl.ds(base + pitch - 4, 8), :],
                 ),
             )
-            tile = jnp.where(at_low, from_low[pl.ds(k, 1), :], tile)
-            tile = jnp.where(at_high, from_high[pl.ds(k, 1), :], tile)
             if f == 0:
-                tile = jnp.where(layer == 5, from_left[pl.ds(y, 1), :], tile)
-                tile = jnp.where(layer == 6, from_right[pl.ds(y, 1), :], tile)
+                tile = jnp.where(layer == 5, west[pl.ds(y, 1), :], tile)
+                tile = jnp.where(layer == 6, east[pl.ds(y, 1), :], tile)
                 tile = jnp.where(layer == 7, z.astype(jnp.float32), tile)
-            if f == 1:
-                tile = jnp.where(layer == 7, y.astype(jnp.float32), tile)
             grab[f, pl.ds(pl.multiple_of(i * 8, 8), 8), :] = tile
         return carry
 
-    lax.fori_loop(0, total, gather, 0, unroll=4)
-
-    source = lax.broadcasted_iota(jnp.int32, (2 * lanes, fields * lanes), 0)
-    target = lane_index((2 * lanes, fields * lanes))
-    wanted = jnp.where(
-        source < lanes, source // depth * lanes, (source - lanes) // depth * lanes + lanes - 1
-    )
-    chooser = jnp.where(target == wanted, 1.0, 0.0).astype(jnp.bfloat16)
+    lax.fori_loop(0, total, gather, 0, unroll=8)
+
+    source = lax.broadcasted_iota(jnp.int32, (2 * lanes, lanes), 0)
+    target = lane_index((2 * lanes, lanes))
+    source = jnp.where(
+        target == 0, source, jnp.where(target == lanes - 1, source - lanes, -1)
+    )
     level = grab[0, pl.ds(7, total, stride=8), :]
     lane = lane_index((total, lanes))
-    own = (lane % depth).astype(jnp.float32) == level
+    own = (lane & (depth - 1)).astype(jnp.float32) == level
     own = own & (lane < fields * depth)
     halo = jnp.concatenate(
         [jnp.where(own, grab[0, pl.ds(5 + c, total, stride=8), :], 0.0) for c in range(2)], 1
@@ -291,16 +303,31 @@
     rest = halo - coarse.astype(jnp.float32)
     middle = rest.astype(jnp.bfloat16)
     fine = (rest - middle.astype(jnp.float32)).astype(jnp.bfloat16)
-    edge[...] = (
-        jnp.dot(coarse, chooser, preferred_element_type=jnp.float32)
-        + jnp.dot(middle, chooser, preferred_element_type=jnp.float32)
-        + jnp.dot(fine, chooser, preferred_element_type=jnp.float32)
-    )
-
-    part = 16
+    for f in range(fields):
+        here = (source >= f * depth) & (source < (f + 1) * depth)
+        chooser = jnp.where(here, 1.0, 0.0).astype(jnp.bfloat16)
+        edge[f] = (
+            jnp.dot(coarse, chooser, preferred_element_type=jnp.float32)
+            + jnp.dot(middle, chooser, preferred_element_type=jnp.float32)
+            + jnp.dot(fine, chooser, preferred_element_type=jnp.float32)
+        )
+
+    def pack_shared(k, carry):
+        slot = jnp.where(rank[k] >= 0, k, 0)
+        row = rank[slot] * block_rows
+        for c in range(6):
+            send[pl.ds(row + c, 1), :] = shared[pl.ds(c * slots + slot, 1), :]
+        return carry
+
+    lax.fori_loop(0, slots, pack_shared, 0, unroll=8)
+
+    part = 32
+
+    def copy_out(g):
+        span = pl.ds(pl.multiple_of(g * part * block_rows, 8), part * block_rows)
+        return pltpu.make_async_copy(send.at[span], send_out.at[span], sems.at[g])
+
     lane = lane_index((part, lanes))
-    west_keep = jnp.where(lane == 0, keep_left, 1.0)
-    east_keep = jnp.where(lane == lanes - 1, keep_right, 1.0)
 
     def advance(g, carry):
         first = pl.multiple_of(g * part, part)
@@ -311,11 +338,8 @@
         def states(k):
             return [rows(f, k) for f in range(fields)]
 
-        z, y = rows(0, 7), rows(1, 7)
         here = states(1)
-        sides = [
-            edge[pl.ds(first, part), f * lanes : (f + 1) * lanes] for f in range(fields)
-        ]
+        sides = [edge[f, pl.ds(first, part), :] for f in range(fields)]
         before = [
             jnp.where(lane == 0, s, pltpu.roll(h, 1, 1)) for s, h in zip(sides, here)
         ]
@@ -324,15 +348,15 @@
             for s, h in zip(sides, here)
         ]
         change = [0.0] * fields
-        for a, b, normal, mask, sign in (
-            (states(3), here, 3, jnp.where(z == 0.0, 0.0, 1.0), -1),
-            (here, states(4), 3, jnp.where(z == depth - 1.0, 0.0, 1.0), 1),
-            (states(0), here, 2, jnp.where(y == 0.0, keep_low, 1.0), -1),
-            (here, states(2), 2, jnp.where(y == height - 1.0, keep_high, 1.0), 1),
-            (before, here, 1, west_keep, -1),
-            (here, after, 1, east_keep, 1),
+        for a, b, normal, sign in (
+            (states(3), here, 3, -1),
+            (here, states(4), 3, 1),
+            (states(0), here, 2, -1),
+            (here, states(2), 2, 1),
+            (before, here, 1, -1),
+            (here, after, 1, 1),
         ):
-            through = fluxes(a, b, normal, mask)
+            through = fluxes(a, b, normal)
             change = [c + t if sign > 0 else c - t for c, t in zip(change, through)]
         density = here[0] - change[0]
         inverse = 1.0 / density
@@ -340,35 +364,48 @@
             value = density if f == 0 else (here[0] * here[f] - change[f]) * inverse
             send[pl.ds(first * block_rows + gas_row + f, part, stride=block_rows), :] = value
             kept[f, pl.ds(first, part), :] = value
+        copy_out(g).start()
         return carry
 
     lax.fori_loop(0, total // part, advance, 0)
 
-    def pack_shared(k, carry):
-        slot = jnp.where(rank[k] >= 0, k, 0)
-        row = rank[slot] * block_rows
-        for c in range(6):
-            send[pl.ds(row + c, 1), :] = shared[pl.ds(c * slots + slot, 1), :]
-        return carry
-
-    lax.fori_loop(0, slots, pack_shared, 0, unroll=8)
-
-
-def occupied(tiles, rank, state, received, shared):
+    for g in range(total // part):
+        copy_out(g).wait()
+
+
+def occupied(tiles, rank, state, own, received, shared):
     total = tiles.shape[1]
     width = state.shape[-1]
+    height = own[0].shape[0]
+    flat = state.reshape(fields, -1, width)
     return pl.pallas_call(
         occupied_kernel,
-        out_shape=(struct(total * block_rows, width), struct(fields, total, width)),
-        in_specs=[smem_spec] * 2 + [vmem_spec] * 6,
-        out_specs=(vmem_spec,) * 2,
+        out_shape=(
+            pltpu.HBM((total * block_rows, width), jnp.float32),
+            struct(fields, total, width),
+            near(*flat.shape),
+        ),
+        in_specs=[smem_spec] * 2 + [vmem_spec] * 8,
+        out_specs=(hbm_spec, vmem_spec, vmem_spec),
         scratch_shapes=[
+            VM((total * block_rows, width), jnp.float32),
             VM((fields, total * 8, width), jnp.float32),
-            VM((total, fields * width), jnp.float32),
+            VM((fields, total, width), jnp.float32),
+            VM((height, width), jnp.float32),
+            VM((height, width), jnp.float32),
+            pltpu.SemaphoreType.DMA((total // 32,)),
         ],
+        input_output_aliases={2: 2},
         compiler_params=params(24),
         name="occupied",
-    )(tiles, rank, state, *received, shared)
+    )(
+        tiles,
+        rank,
+        pltpu.with_memory_space_constraint(flat, pltpu.VMEM),
+        *own,
+        *received,
+        shared,
+    )[:2]
 
 
 def advect_kernel(
@@ -582,14 +619,17 @@
     slots = rank.shape[0]
     part = 32
 
+    def inside(c):
+        return gas.at[c, pl.ds(0, cells)].reshape(depth, height, width)
+
     def load(c):
         return pltpu.make_async_copy(
-            advanced.at[1 + c], gas.at[c, pl.ds(0, depth)], in_sems.at[c]
+            advanced.at[1 + c], inside(c), in_sems.at[c]
         )
 
     def store(c):
         return pltpu.make_async_copy(
-            gas.at[c, pl.ds(0, depth)], gas_out.at[1 + c], out_sems.at[c]
+            inside(c), gas_out.at[1 + c], out_sems.at[c]
         )
 
     for c in range(4):
@@ -614,9 +654,8 @@
     def scatter(i, carry):
         block = tiles[0, i]
         block = jnp.where(block >= 0, block, cells)
-        z = quotient(block, height, cells + 1)
         for c in range(4):
-            gas[c, z, pl.ds(block - z * height, 1), :] = fresh[c, pl.ds(i, 1), :]
+            gas[c, pl.ds(block, 1), :] = fresh[c, pl.ds(i, 1), :]
         return carry
 
     lax.fori_loop(0, total, scatter, 0, unroll=8)
@@ -658,7 +697,7 @@
         in_specs=[smem_spec] * 2 + [vmem_spec] * 2 + [hbm_spec] + [vmem_spec] * 2,
         out_specs=(hbm_spec, vmem_spec),
         scratch_shapes=[
-            VM((4, depth + 1, height, width), jnp.float32),
+            VM((4, depth * height + 8, width), jnp.float32),
             VM((4, total, width), jnp.float32),
             VM((fields, slots, width), jnp.float32),
             pltpu.SemaphoreType.DMA((4,)),
@@ -705,7 +744,9 @@
         grain_voxel_number,
         grain_substance_label,
     )
-    send, kept = occupied(sender_tile_map, receiver_arrival_rank, state, received, shared)
+    send, kept = occupied(
+        sender_tile_map, receiver_arrival_rank, state, (left, right), received, shared
+    )
     devices = lax.axis_size("gx") * lax.axis_size("gy")
     width = send.shape[-1]
     arrived = lax.all_to_all(

time: 63.9 us -> 56.9 us (0.89)
  Pallas kernels: 34.5 us -> 27.3 us
  waiting for transfers between devices: 13.3 us -> 14.3 us
  starting transfers between devices: 15 us -> 14.2 us
    pallas_call x1, Pallas kernels: 8.53 us -> 5.15 us  [occupied(): pl.pallas_call(occupied_kernel, out_shape=(pltpu.HBM((total * block_rows,...]
    pallas_call x1, Pallas kernels: 5.42 us -> 3.69 us  [binning(): pl.pallas_call(binning_kernel, out_shape=(struct(6 * slots, lanes), struc...]
    pallas_call x1, Pallas kernels: 6.73 us -> 5.45 us  [exchange(): pl.pallas_call(exchange_kernel, out_shape=(pltpu.HBM(advanced.shape, jnp....]
    ppermute x4, waiting for transfers between devices: 0.01 us -> 0.93 us  [shifted(): lax.ppermute(array, axis, [(i, (i + step) % count) for i in range(count)])]
    all_to_all x1, starting transfers between devices: 6.34 us -> 5.52 us  [per_device(): lax.all_to_all(send.reshape(devices, block_rows, -1, width), ('gx', 'gy')...]
    pallas_call x1, Pallas kernels: 4.06 us -> 3.27 us  [edges(): pl.pallas_call(edges_kernel, out_shape=(struct(height, width), struct(hei...]
  transfers between devices with their start and end apart: 5 -> 5, of which waited for: 1 -> 2; matrix products, arithmetic and copies ran while one was open for 0% -> 0% of each run, Pallas kernels for 24% -> 24%
where the time goes in v2:
time: 56.9 us; the launch traced here: 56.6 us
  Pallas kernels  27.3 us (48%)
  waiting for transfers between devices  14.3 us (25%)
  starting transfers between devices  14.2 us (25%)
  between operations  0.81 us (1%)
    all_to_all x1, waiting for transfers between devices, per_device(): lax.all_to_all(send.reshape(devices, block_rows, -1, width), ('gx', 'gy')...  13.4 us
    pallas_call x1, Pallas kernels, advect(): pl.pallas_call(advect_kernel, out_shape=pltpu.HBM((fields, depth, height,...  9.71 us
    ppermute x4, starting transfers between devices, shifted(): lax.ppermute(array, axis, [(i, (i + step) % count) for i in range(count)])  8.64 us
    all_to_all x1, starting transfers between devices, per_device(): lax.all_to_all(send.reshape(devices, block_rows, -1, width), ('gx', 'gy')...  5.52 us
    pallas_call x1, Pallas kernels, exchange(): pl.pallas_call(exchange_kernel, out_shape=(pltpu.HBM(advanced.shape, jnp....  5.45 us
    pallas_call x1, Pallas kernels, occupied(): pl.pallas_call(occupied_kernel, out_shape=(pltpu.HBM((total * block_rows,...  5.15 us
    pallas_call x1, Pallas kernels, binning(): pl.pallas_call(binning_kernel, out_shape=(struct(6 * slots, lanes), struc...  3.69 us
    pallas_call x1, Pallas kernels, edges(): pl.pallas_call(edges_kernel, out_shape=(struct(height, width), struct(hei...  3.27 us
  transfers between devices with their start and end apart: 5, of which 2 were waited for; matrix products, arithmetic and copies ran while one was open for 0% of the time, Pallas kernels for 24%

profile of v2, /device:TPU:0, one launch (start us, length us, event | category | flops | bytes accessed | tf_op | source)
XLA Modules:
  0.0 56.6 jit_solution(8045417655490006541)
XLA Ops:
  0.6 0.0 copy-start.7
  0.6 0.0 copy-start.6
  0.7 0.0 copy-start.5
  0.7 0.0 copy-start.4
  0.7 0.0 copy-start.2
  0.7 0.0 copy-start.3
  0.7 0.0 copy-start.8
  0.7 3.3 %edges.1 = (f32[96,128]{1,0:T(8,128)S(1)}, f32[96,128]{1,0:T(8,128)S(1)}, f32[80,128]{1,0:T(8,128)S(1)}, f32[80,128]{1,0:T(8,128)S(1)}, f32[5,18,112,128]{3,2,1,0:T(8,128)S(1)}) custom-call(f32[16,96,128]{2,1,0:T(8,128)} %rho.3, f32[3,16,96,128]{3,2,1,0:T(8,128)} %flow.5, f32[16,96,128]{2,1,0:T(8,128)} %kelvin.5), custom_call_target="tpu_custom_call" | custom-call | tf_op jit(solution)/shard_map/edges/pallas_call | solution.py:92
  4.0 1.7 %collective-permute-start.2 = (f32[80,128]{1,0:T(8,128)S(1)}, f32[80,128]{1,0:T(8,128)S(1)}, u32[]{:S(2)}, u32[]{:S(2)}) collective-permute-start(f32[80,128]{1,0:T(8,128)S(1)} %get-tuple-element.16), channel_id=1, source_target_pairs={{0,1},{1,2},{2,3},{3,4},{4,5},{5,6},{6,7},{7,8},{8,9},{9,10},{10,1... | collective-permute-start | bytes 122888 | tf_op jit(solution)/shard_map/ppermute | solution.py:730
  5.7 3.7 %collective-permute-start.3 = (f32[80,128]{1,0:T(8,128)S(1)}, f32[80,128]{1,0:T(8,128)S(1)}, u32[]{:S(2)}, u32[]{:S(2)}) collective-permute-start(f32[80,128]{1,0:T(8,128)S(1)} %get-tuple-element.17), channel_id=1, source_target_pairs={{0,15},{1,0},{2,1},{3,2},{4,3},{5,4},{6,5},{7,6},{8,7},{9,8},{10,9... | collective-permute-start | bytes 122888 | tf_op jit(solution)/shard_map/ppermute | solution.py:730
  9.4 3.2 %collective-permute-start.1 = (f32[96,128]{1,0:T(8,128)S(1)}, f32[96,128]{1,0:T(8,128)S(1)}, u32[]{:S(2)}, u32[]{:S(2)}) collective-permute-start(f32[96,128]{1,0:T(8,128)S(1)} %get-tuple-element.14.own_left), channel_id=1, source_target_pairs={{0,112},{16,0},{32,16},{48,32},{64,48},{80,64},{96,80},{112,96},{1... | collective-permute-start | bytes 147464 | tf_op jit(solution)/shard_map/ppermute | solution.py:730
  12.6 0.0 copy-start
  12.6 0.0 copy-start.1
  12.6 0.0 collective-permute-start
  12.6 0.0 copy-done.7
  12.6 0.0 copy-done.6
  12.6 0.0 copy-done.5
  12.7 0.0 copy-done.4
  12.7 0.0 copy-done.2
  12.7 0.0 copy-done.3
  12.7 0.0 copy-done.8
  12.7 3.7 %binning.1 = (f32[384,128]{1,0:T(8,128)S(1)}, f32[768,128]{1,0:T(8,128)S(1)}) custom-call(s32[64]{0:T(128)S(1)} %copy-done.8, f32[2,2]{1,0:T(2,128)S(1)} %copy-done.7, f32[64,512]{1,0:T(8,128)S(1)} %copy-done.3, f32[3,64,512]{2,1,0:T(8,128)S(1)} %copy-done.2, f32[64,512]{1,0:T(8,128)S(1)} %copy-done.4, s32[64,512]{1,0:T(8,128)S(1)} %copy-done.5, ...), custom_call_target="tpu_custom_call" | custom-call | flops 4000000000 | bytes 12000000 | tf_op jit(solution)/shard_map/binning/pallas_call | solution.py:181
  16.4 0.0 collective-permute-done.2.from_low
  16.4 0.0 collective-permute-done.3.from_high
  16.4 0.0 collective-permute-done.1.from_right
  16.4 0.9 %collective-permute-done.from_left = f32[96,128]{1,0:T(8,128)S(1)} collective-permute-done((f32[96,128]{1,0:T(8,128)S(1)}, f32[96,128]{1,0:T(8,128)S(1)}, u32[]{:S(2)}, u32[]{:S(2)}) %collective-permute-start) | collective-permute-done | bytes 49184 | tf_op jit(solution)/shard_map/ppermute | solution.py:730
  17.3 0.0 copy-done
  17.4 0.0 copy-done.1
  17.4 5.2 %occupied.1 = (f32[2816,128]{1,0:T(8,128)}, f32[5,256,128]{2,1,0:T(8,128)S(1)}, f32[5,2016,128]{2,1,0:T(8,128)S(1)}) custom-call(s32[1,256]{1,0:T(1,128)S(1)} %copy-done, s32[64]{0:T(128)S(1)} %copy-done.1, f32[5,2016,128]{2,1,0:T(8,128)S(1)} %bitcast.5, f32[96,128]{1,0:T(8,128)S(1)} %get-tuple-element.14.own_left, ...), custom_call_target="tpu_custom_call", output_to_operand_aliasing={{2}: (2, {})} | custom-call | tf_op jit(solution)/shard_map/occupied/pallas_call | solution.py:381
  22.5 5.5 %all-to-all-start = ((f32[128,11,2,128]{3,2,1,0:T(2,128)}), f32[128,11,2,128]{3,2,1,0:T(2,128)S(1)}, u32[]{:S(2)}, u32[]{:S(2)}) async-start(f32[128,11,2,128]{3,2,1,0:T(2,128)} %bitcast.6), calls=%async_computation | async-start | bytes 2883584 | tf_op jit(solution)/shard_map/all_to_all | solution.py:752
  28.0 9.7 %advect.1.advanced = f32[5,16,96,128]{3,2,1,0:T(8,128)} custom-call(f32[16,96,128]{2,1,0:T(8,128)} %rho.3, f32[3,16,96,128]{3,2,1,0:T(8,128)} %flow.5, f32[16,96,128]{2,1,0:T(8,128)} %kelvin.5, f32[96,128]{1,0:T(8,128)S(1)} %get-tuple-element.14.own_left, f32[96,128]{1,0:T(8,128)S(1)} %get-tuple-element.15.own_right, ...), custom_call_target="tpu_custom_call" | custom-call | flops 4000000000 | bytes 12000000 | tf_op jit(solution)/shard_map/advect/pallas_call | solution.py:569
  37.8 13.4 %all-to-all-done = f32[128,11,2,128]{3,2,1,0:T(2,128)S(1)} async-done(((f32[128,11,2,128]{3,2,1,0:T(2,128)}), f32[128,11,2,128]{3,2,1,0:T(2,128)S(1)}, u32[]{:S(2)}, u32[]{:S(2)}) %all-to-all-start) | async-done | bytes 1441824 | tf_op jit(solution)/shard_map/all_to_all | solution.py:752
  51.2 5.5 %exchange.1 = (f32[5,16,96,128]{3,2,1,0:T(8,128)}, f32[4,128,128]{2,1,0:T(8,128)}) custom-call(s32[1,256]{1,0:T(1,128)S(1)} %copy-done, s32[64]{0:T(128)S(1)} %copy-done.1, f32[2816,128]{1,0:T(8,128)S(1)} %bitcast.4, f32[5,256,128]{2,1,0:T(8,128)S(1)} %get-tuple-element.20.kept, f32[5,16,96,128]{3,2,1,0:T(8,128)} %advect.1.advanced, ...), custom_call_target="tpu_custom_call", output_to_operand_aliasing={{0}: (4, {})} | custom-call | tf_op jit(solution)/shard_map/exchange/pallas_call | solution.py:694
Async XLA Ops:
  0.6 12.0 %copy-start.7 = (f32[2,2]{1,0:T(2,128)S(1)}, f32[2,2]{1,0:T(2,128)}, u32[]{:S(2)}) copy-start(f32[2,2]{1,0:T(2,128)} %factor.1) | copy-start | bytes 52
  0.6 12.0 %copy-start.6 = (s32[64,512]{1,0:T(8,128)S(1)}, s32[64,512]{1,0:T(8,128)}, u32[]{:S(2)}) copy-start(s32[64,512]{1,0:T(8,128)} %label.1) | copy-start | bytes 393220
  0.7 12.0 %copy-start.5 = (s32[64,512]{1,0:T(8,128)S(1)}, s32[64,512]{1,0:T(8,128)}, u32[]{:S(2)}) copy-start(s32[64,512]{1,0:T(8,128)} %cell.1) | copy-start | bytes 393220
  0.7 12.0 %copy-start.4 = (f32[64,512]{1,0:T(8,128)S(1)}, f32[64,512]{1,0:T(8,128)}, u32[]{:S(2)}) copy-start(f32[64,512]{1,0:T(8,128)} %kelvin.4) | copy-start | bytes 393220
  0.7 12.0 %copy-start.2 = (f32[3,64,512]{2,1,0:T(8,128)S(1)}, f32[3,64,512]{2,1,0:T(8,128)}, u32[]{:S(2)}) copy-start(f32[3,64,512]{2,1,0:T(8,128)} %flow.4) | copy-start | bytes 1179652
  0.7 12.0 %copy-start.3 = (f32[64,512]{1,0:T(8,128)S(1)}, f32[64,512]{1,0:T(8,128)}, u32[]{:S(2)}) copy-start(f32[64,512]{1,0:T(8,128)} %mass.1) | copy-start | bytes 393220
  0.7 12.0 %copy-start.8 = (s32[64]{0:T(128)S(1)}, s32[64]{0:T(128)}, u32[]{:S(2)}) copy-start(s32[64]{0:T(128)} %count.1) | copy-start | bytes 772
  4.0 12.4 %collective-permute-start.2 = (f32[80,128]{1,0:T(8,128)S(1)}, f32[80,128]{1,0:T(8,128)S(1)}, u32[]{:S(2)}, u32[]{:S(2)}) collective-permute-start(f32[80,128]{1,0:T(8,128)S(1)} %get-tuple-element.16), channel_id=1, source_target_pairs={{0,1},{1,2},{2,3},{3,4},{4,5},{5,6},{6,7},{7,8},{8,9},{9,10},{10,1... | collective-permute-start | bytes 122888 | tf_op jit(solution)/shard_map/ppermute | solution.py:730
  5.7 10.7 %collective-permute-start.3 = (f32[80,128]{1,0:T(8,128)S(1)}, f32[80,128]{1,0:T(8,128)S(1)}, u32[]{:S(2)}, u32[]{:S(2)}) collective-permute-start(f32[80,128]{1,0:T(8,128)S(1)} %get-tuple-element.17), channel_id=1, source_target_pairs={{0,15},{1,0},{2,1},{3,2},{4,3},{5,4},{6,5},{7,6},{8,7},{9,8},{10,9... | collective-permute-start | bytes 122888 | tf_op jit(solution)/shard_map/ppermute | solution.py:730
  9.4 7.0 %collective-permute-start.1 = (f32[96,128]{1,0:T(8,128)S(1)}, f32[96,128]{1,0:T(8,128)S(1)}, u32[]{:S(2)}, u32[]{:S(2)}) collective-permute-start(f32[96,128]{1,0:T(8,128)S(1)} %get-tuple-element.14.own_left), channel_id=1, source_target_pairs={{0,112},{16,0},{32,16},{48,32},{64,48},{80,64},{96,80},{112,96},{1... | collective-permute-start | bytes 147464 | tf_op jit(solution)/shard_map/ppermute | solution.py:730
  12.6 4.7 %copy-start = (s32[1,256]{1,0:T(1,128)S(1)}, s32[1,256]{1,0:T(1,128)}, u32[]{:S(2)}) copy-start(s32[1,256]{1,0:T(1,128)} %tiles.3) | copy-start | bytes 3076
  12.6 4.7 %copy-start.1 = (s32[64]{0:T(128)S(1)}, s32[64]{0:T(128)}, u32[]{:S(2)}) copy-start(s32[64]{0:T(128)} %rank.3) | copy-start | bytes 772
  12.6 4.7 %collective-permute-start = (f32[96,128]{1,0:T(8,128)S(1)}, f32[96,128]{1,0:T(8,128)S(1)}, u32[]{:S(2)}, u32[]{:S(2)}) collective-permute-start(f32[96,128]{1,0:T(8,128)S(1)} %get-tuple-element.15.own_right), channel_id=1, source_target_pairs={{0,16},{16,32},{32,48},{48,64},{64,80},{80,96},{96,112},{112,0},{1... | collective-permute-start | bytes 147464 | tf_op jit(solution)/shard_map/ppermute | solution.py:730
  22.5 28.6 %all-to-all-start = ((f32[128,11,2,128]{3,2,1,0:T(2,128)}), f32[128,11,2,128]{3,2,1,0:T(2,128)S(1)}, u32[]{:S(2)}, u32[]{:S(2)}) async-start(f32[128,11,2,128]{3,2,1,0:T(2,128)} %bitcast.6), calls=%async_computation | async-start | bytes 2883584 | tf_op jit(solution)/shard_map/all_to_all | solution.py:752

commit v3 on v2

--- a/solution.py
+++ b/solution.py
@@ -12,7 +12,10 @@
 row_pad = 8
 block_rows = 11
 gas_row = 6
+exchange_pieces = 1
+group_fields = 2
 row_chunk = 16
+advance_part = 32
 
 VM = pltpu.VMEM
 vmem_spec = pl.BlockSpec(memory_space=pltpu.VMEM)
@@ -41,45 +44,71 @@
     return lax.broadcasted_iota(jnp.int32, shape, len(shape) - 1)
 
 
-def edges_kernel(rho, flow, kelvin, left, right, low, high, held, sems):
+def is_even(axis):
+    return lax.axis_index(axis) % 2 == 0
+
+
+def swapped(array, axis, second):
+    count = lax.axis_size(axis)
+    assert count % 2 == 0
+    pairs = [(i, i ^ 1) for i in range(count)]
+    if second:
+        pairs = [((i + 1) % count, (j + 1) % count) for i, j in pairs]
+    return lax.ppermute(array, axis, pairs)
+
+
+def edges_kernel(rho, flow, kelvin, left, right, x_one, x_two, y_one, y_two, held, sems):
     depth, height, _ = rho.shape
     parts = sems.shape[1]
-    rows = height // parts
+    planes = depth // parts
+    rows = 24
+    inner = pl.ds(row_pad, height)
 
     def copies(part):
-        span = pl.ds(part * rows, rows)
-        into = pl.ds(row_pad + part * rows, rows)
+        span = pl.ds(part * planes, planes)
+        into = pl.ds(1 + part * planes, planes)
         return [
-            pltpu.make_async_copy(rho.at[:, span], held.at[0, pl.ds(1, depth), into], sems.at[0, part]),
-            pltpu.make_async_copy(flow.at[:, :, span], held.at[1:4, pl.ds(1, depth), into], sems.at[1, part]),
-            pltpu.make_async_copy(kelvin.at[:, span], held.at[4, pl.ds(1, depth), into], sems.at[2, part]),
+            pltpu.make_async_copy(rho.at[span], held.at[0, into, inner], sems.at[0, part]),
+            pltpu.make_async_copy(flow.at[:, span], held.at[1:4, into, inner], sems.at[1, part]),
+            pltpu.make_async_copy(kelvin.at[span], held.at[4, into, inner], sems.at[2, part]),
         ]
 
     for part in range(parts):
         for copy in copies(part):
             copy.start()
     lane = lane_index((rows, lanes))
+    even_x, even_y = is_even("gx"), is_even("gy")
     for part in range(parts):
         for copy in copies(part):
             copy.wait()
-
-        span = pl.ds(part * rows, rows)
-        inside = pl.ds(row_pad + part * rows, rows)
-        first = jnp.zeros((rows, lanes), jnp.float32)
-        last = jnp.zeros((rows, lanes), jnp.float32)
-        for f in range(fields):
-            for z in range(depth):
-                k = f * depth + z
-                turned = pltpu.roll(held[f, z + 1, inside, :], k + 1, 1)
-                last = jnp.where(lane == k, turned, last)
-                first = jnp.where(lane == k + 1, turned, first)
-        left[span, :] = pltpu.roll(first, lanes - 1, 1)
-        right[span, :] = last
+        for start in range(0, height, rows):
+            span = pl.ds(start, rows)
+            inside = pl.ds(row_pad + start, rows)
+            if part == 0:
+                first = jnp.zeros((rows, lanes), jnp.float32)
+                last = jnp.zeros((rows, lanes), jnp.float32)
+            else:
+                first, last = left[span, :], right[span, :]
+            for f in range(fields):
+                for z in range(part * planes, (part + 1) * planes):
+                    k = f * depth + z
+                    turned = pltpu.roll(held[f, z + 1, inside, :], k + 1, 1)
+                    last = jnp.where(lane == k, turned, last)
+                    first = jnp.where(lane == k + 1, turned, first)
+            if part == parts - 1:
+                first = pltpu.roll(first, lanes - 1, 1)
+            left[span, :] = first
+            right[span, :] = last
+            if part == parts - 1:
+                x_one[span, :] = jnp.where(even_x, last, first)
+                x_two[span, :] = jnp.where(even_x, first, last)
     for f in range(fields):
         for z in range(depth):
             k = f * depth + z
-            low[k : k + 1, :] = held[f, z + 1, row_pad : row_pad + 1, :]
-            high[k : k + 1, :] = held[f, z + 1, row_pad + height - 1 : row_pad + height, :]
+            low = held[f, z + 1, row_pad : row_pad + 1, :]
+            high = held[f, z + 1, row_pad + height - 1 : row_pad + height, :]
+            y_one[k : k + 1, :] = jnp.where(even_y, high, low)
+            y_two[k : k + 1, :] = jnp.where(even_y, low, high)
     for f in range(fields):
         sign = -1.0 if f == 3 else 1.0
         held[f, 0] = sign * held[f, 1]
@@ -94,12 +123,14 @@
         out_shape=(
             struct(height, width),
             struct(height, width),
+            struct(height, width),
+            struct(height, width),
             struct(fields * depth, width),
             struct(fields * depth, width),
             near(fields, depth + 2, height + 2 * row_pad, width),
         ),
         in_specs=[hbm_spec] * 3,
-        out_specs=(vmem_spec,) * 5,
+        out_specs=(vmem_spec,) * 7,
         scratch_shapes=[
             pltpu.SemaphoreType.DMA((3, parts)),
         ],
@@ -108,7 +139,9 @@
     )(*in_hbm(rho, flow, kelvin))
 
 
-def binning_kernel(count, factor, mass, flow, kelvin, cell, label, shared, solid, held, sums):
+def binning_kernel(
+    count, factor, rank, mass, flow, kelvin, cell, label, shared, packed, solid, held, sums
+):
     slots, padding = mass.shape
     width = lanes
 
@@ -175,14 +208,27 @@
     for c in range(6):
         shared[c * slots : (c + 1) * slots, :] = totals[c]
 
-
-def binning(count, factor, mass, flow, kelvin, cell, label):
+    def pack(k, carry):
+        slot = jnp.where(rank[k] >= 0, k, 0)
+        row = rank[slot]
+        for c in range(6):
+            packed[c, pl.ds(row, 1), :] = shared[pl.ds(c * slots + slot, 1), :]
+        return carry
+
+    lax.fori_loop(0, slots, pack, 0, unroll=16)
+
+
+def binning(count, factor, rank, total, mass, flow, kelvin, cell, label):
     slots, padding = mass.shape
     return pl.pallas_call(
         binning_kernel,
-        out_shape=(struct(6 * slots, lanes), struct(12 * slots, lanes)),
-        in_specs=[smem_spec] * 2 + [vmem_spec] * 5,
-        out_specs=(vmem_spec,) * 2,
+        out_shape=(
+            struct(6 * slots, lanes),
+            struct(6, total, lanes),
+            struct(12 * slots, lanes),
+        ),
+        in_specs=[smem_spec] * 3 + [vmem_spec] * 5,
+        out_specs=(vmem_spec,) * 3,
         scratch_shapes=[
             VM((padding // lanes, slots * 8, lanes), jnp.float32),
             VM((slots * 16, lanes), jnp.float32),
@@ -192,7 +238,7 @@
         ),
         compiler_params=params(16),
         name="binning",
-    )(count, factor, mass, flow, kelvin, cell, label)
+    )(count, factor, rank, mass, flow, kelvin, cell, label)
 
 
 def fluxes(a, b, normal, keep=None):
@@ -215,15 +261,14 @@
 
 def occupied_kernel(
     tiles,
-    rank,
     _,
     own_left,
     own_right,
-    from_left,
-    from_right,
-    from_low,
-    from_high,
-    shared,
+    x_one,
+    x_two,
+    y_one,
+    y_two,
+    packed,
     send_out,
     kept,
     state,
@@ -235,11 +280,11 @@
     sems,
 ):
     total = tiles.shape[1]
-    slots = rank.shape[0]
-    height = from_left.shape[0]
-    depth = from_low.shape[0] // fields
+    height = own_left.shape[0]
+    depth = y_one.shape[0] // fields
     pitch = height + 2 * row_pad
     gx, gy = lax.axis_index("gx"), lax.axis_index("gy")
+    even_x, even_y = is_even("gx"), is_even("gy")
 
     def walled(wall, f, normal, own, other):
         return jnp.where(wall, -own if f == normal else own, other)
@@ -249,16 +294,26 @@
             k = slice(f * depth + z, f * depth + z + 1)
             row = (z + 1) * pitch + row_pad
             state[f, row - 1 : row, :] = walled(
-                gy == 0, f, 2, state[f, row : row + 1, :], from_low[k, :]
+                gy == 0,
+                f,
+                2,
+                state[f, row : row + 1, :],
+                jnp.where(even_y, y_two[k, :], y_one[k, :]),
             )
             row = row + height - 1
             state[f, row + 1 : row + 2, :] = walled(
-                gy == lax.axis_size("gy") - 1, f, 2, state[f, row : row + 1, :], from_high[k, :]
+                gy == lax.axis_size("gy") - 1,
+                f,
+                2,
+                state[f, row : row + 1, :],
+                jnp.where(even_y, y_one[k, :], y_two[k, :]),
             )
     lane = lane_index((height, lanes))
     sign = jnp.where((lane >= depth) & (lane < 2 * depth), -1.0, 1.0)
-    west[...] = jnp.where(gx == 0, sign * own_left[...], from_left[...])
-    east[...] = jnp.where(gx == lax.axis_size("gx") - 1, sign * own_right[...], from_right[...])
+    from_left = jnp.where(even_x, x_two[...], x_one[...])
+    from_right = jnp.where(even_x, x_one[...], x_two[...])
+    west[...] = jnp.where(gx == 0, sign * own_left[...], from_left)
+    east[...] = jnp.where(gx == lax.axis_size("gx") - 1, sign * own_right[...], from_right)
 
     assert depth & (depth - 1) == 0
     layer = lax.broadcasted_iota(jnp.int32, (8, lanes), 0)
@@ -285,7 +340,7 @@
             grab[f, pl.ds(pl.multiple_of(i * 8, 8), 8), :] = tile
         return carry
 
-    lax.fori_loop(0, total, gather, 0, unroll=8)
+    lax.fori_loop(0, total, gather, 0, unroll=16)
 
     source = lax.broadcasted_iota(jnp.int32, (2 * lanes, lanes), 0)
     target = lane_index((2 * lanes, lanes))
@@ -300,28 +355,15 @@
         [jnp.where(own, grab[0, pl.ds(5 + c, total, stride=8), :], 0.0) for c in range(2)], 1
     )
     coarse = halo.astype(jnp.bfloat16)
-    rest = halo - coarse.astype(jnp.float32)
-    middle = rest.astype(jnp.bfloat16)
-    fine = (rest - middle.astype(jnp.float32)).astype(jnp.bfloat16)
+    fine = (halo - coarse.astype(jnp.float32)).astype(jnp.bfloat16)
     for f in range(fields):
         here = (source >= f * depth) & (source < (f + 1) * depth)
         chooser = jnp.where(here, 1.0, 0.0).astype(jnp.bfloat16)
-        edge[f] = (
-            jnp.dot(coarse, chooser, preferred_element_type=jnp.float32)
-            + jnp.dot(middle, chooser, preferred_element_type=jnp.float32)
-            + jnp.dot(fine, chooser, preferred_element_type=jnp.float32)
+        edge[f] = jnp.dot(coarse, chooser, preferred_element_type=jnp.float32) + jnp.dot(
+            fine, chooser, preferred_element_type=jnp.float32
         )
 
-    def pack_shared(k, carry):
-        slot = jnp.where(rank[k] >= 0, k, 0)
-        row = rank[slot] * block_rows
-        for c in range(6):
-            send[pl.ds(row + c, 1), :] = shared[pl.ds(c * slots + slot, 1), :]
-        return carry
-
-    lax.fori_loop(0, slots, pack_shared, 0, unroll=8)
-
-    part = 32
+    part = advance_part
 
     def copy_out(g):
         span = pl.ds(pl.multiple_of(g * part * block_rows, 8), part * block_rows)
@@ -360,6 +402,10 @@
             change = [c + t if sign > 0 else c - t for c, t in zip(change, through)]
         density = here[0] - change[0]
         inverse = 1.0 / density
+        for c in range(6):
+            send[pl.ds(first * block_rows + c, part, stride=block_rows), :] = packed[
+                c, pl.ds(first, part), :
+            ]
         for f in range(fields):
             value = density if f == 0 else (here[0] * here[f] - change[f]) * inverse
             send[pl.ds(first * block_rows + gas_row + f, part, stride=block_rows), :] = value
@@ -373,7 +419,7 @@
         copy_out(g).wait()
 
 
-def occupied(tiles, rank, state, own, received, shared):
+def occupied(tiles, state, own, received, packed):
     total = tiles.shape[1]
     width = state.shape[-1]
     height = own[0].shape[0]
@@ -385,7 +431,7 @@
             struct(fields, total, width),
             near(*flat.shape),
         ),
-        in_specs=[smem_spec] * 2 + [vmem_spec] * 8,
+        in_specs=[smem_spec] + [vmem_spec] * 8,
         out_specs=(hbm_spec, vmem_spec, vmem_spec),
         scratch_shapes=[
             VM((total * block_rows, width), jnp.float32),
@@ -393,18 +439,17 @@
             VM((fields, total, width), jnp.float32),
             VM((height, width), jnp.float32),
             VM((height, width), jnp.float32),
-            pltpu.SemaphoreType.DMA((total // 32,)),
+            pltpu.SemaphoreType.DMA((total // advance_part,)),
         ],
-        input_output_aliases={2: 2},
+        input_output_aliases={1: 2},
         compiler_params=params(24),
         name="occupied",
     )(
         tiles,
-        rank,
         pltpu.with_memory_space_constraint(flat, pltpu.VMEM),
         *own,
         *received,
-        shared,
+        packed,
     )[:2]
 
 
@@ -414,10 +459,10 @@
     kelvin,
     own_left,
     own_right,
-    from_left,
-    from_right,
-    from_low,
-    from_high,
+    x_one,
+    x_two,
+    y_one,
+    y_two,
     gas_out,
     state,
     gas,
@@ -431,6 +476,7 @@
 ):
     depth, height, width = rho.shape
     gx, gy = lax.axis_index("gx"), lax.axis_index("gy")
+    even_x, even_y = is_even("gx"), is_even("gy")
 
     def keep(wall):
         return jnp.where(wall, 0.0, 1.0).astype(jnp.float32)
@@ -466,7 +512,7 @@
         span = pl.ds(pl.multiple_of(g * 8, 8), 8)
 
         def split(left_faces, right_faces):
-            at_left, at_right = left_faces[span, :], right_faces[span, :]
+            at_left, at_right = left_faces, right_faces
             parts = []
             for f in range(fields):
                 one = pltpu.roll(at_left, (lanes - f * depth) % lanes, 1)
@@ -474,7 +520,14 @@
                 parts.append(jnp.where(narrow < depth, one, two))
             return parts
 
-        through = fluxes(split(from_left, own_right), split(own_left, from_right), 1, keep_sides)
+        from_left = jnp.where(even_x, x_two[span, :], x_one[span, :])
+        from_right = jnp.where(even_x, x_one[span, :], x_two[span, :])
+        through = fluxes(
+            split(from_left, own_right[span, :]),
+            split(own_left[span, :], from_right),
+            1,
+            keep_sides,
+        )
         for f in range(fields):
             whole = jnp.where(narrow < 2 * depth, through[f], 0.0)
             coarse = whole.astype(jnp.bfloat16).astype(jnp.float32)
@@ -511,8 +564,9 @@
         edge_flux[...] = jnp.dot(side_parts[...], place, preferred_element_type=jnp.float32)
         for f in range(fields):
             k = f * depth + z
-            state[f, z, row_pad - 1 : row_pad, :] = from_low[pl.ds(k, 1), :]
-            state[f, z, row_pad + height : row_pad + height + 1, :] = from_high[pl.ds(k, 1), :]
+            one, two = y_one[pl.ds(k, 1), :], y_two[pl.ds(k, 1), :]
+            state[f, z, row_pad - 1 : row_pad, :] = jnp.where(even_y, two, one)
+            state[f, z, row_pad + height : row_pad + height + 1, :] = jnp.where(even_y, one, two)
 
         def faces_y(start, rows):
             a = [state[f, z, pl.ds(row_pad - 1 + start, rows), :] for f in range(fields)]
@@ -619,21 +673,26 @@
     slots = rank.shape[0]
     part = 32
 
-    def inside(c):
-        return gas.at[c, pl.ds(0, cells)].reshape(depth, height, width)
-
-    def load(c):
+    pieces = in_sems.shape[1]
+    planes = depth // pieces
+
+    def inside(c, p):
+        rows = pl.ds(p * planes * height, planes * height)
+        return gas.at[c, rows].reshape(planes, height, width)
+
+    def load(c, p):
         return pltpu.make_async_copy(
-            advanced.at[1 + c], inside(c), in_sems.at[c]
+            advanced.at[1 + c, pl.ds(p * planes, planes)], inside(c, p), in_sems.at[c, p]
         )
 
-    def store(c):
+    def store(c, p):
         return pltpu.make_async_copy(
-            inside(c), gas_out.at[1 + c], out_sems.at[c]
+            inside(c, p), gas_out.at[1 + c, pl.ds(p * planes, planes)], out_sems.at[c, p]
         )
 
     for c in range(4):
-        load(c).start()
+        for p in range(pieces):
+            load(c, p).start()
 
     def blocks(g, carry):
         first = pl.multiple_of(g * part, part)
@@ -648,19 +707,23 @@
         return carry
 
     lax.fori_loop(0, total // part, blocks, 0)
-    for c in range(4):
-        load(c).wait()
-
-    def scatter(i, carry):
-        block = tiles[0, i]
-        block = jnp.where(block >= 0, block, cells)
-        for c in range(4):
-            gas[c, pl.ds(block, 1), :] = fresh[c, pl.ds(i, 1), :]
-        return carry
-
-    lax.fori_loop(0, total, scatter, 0, unroll=8)
-    for c in range(4):
-        store(c).start()
+    for pair in range(0, 4, group_fields):
+        chosen = range(pair, pair + group_fields)
+        for c in chosen:
+            for p in range(pieces):
+                load(c, p).wait()
+
+        def scatter(i, carry):
+            block = tiles[0, i]
+            block = jnp.where(block >= 0, block, cells)
+            for c in chosen:
+                gas[c, pl.ds(block, 1), :] = fresh[c, pl.ds(i, 1), :]
+            return carry
+
+        lax.fori_loop(0, total, scatter, 0, unroll=16)
+        for c in chosen:
+            for p in range(pieces):
+                store(c, p).start()
 
     def gather(k, live):
         spot = rank[k]
@@ -684,7 +747,8 @@
                 alive, base + scale * result[c], 0.0
             )
     for c in range(4):
-        store(c).wait()
+        for p in range(pieces):
+            store(c, p).wait()
 
 
 def exchange(tiles, rank, received, kept, advanced, shared, solid):
@@ -700,8 +764,8 @@
             VM((4, depth * height + 8, width), jnp.float32),
             VM((4, total, width), jnp.float32),
             VM((fields, slots, width), jnp.float32),
-            pltpu.SemaphoreType.DMA((4,)),
-            pltpu.SemaphoreType.DMA((4,)),
+            pltpu.SemaphoreType.DMA((4, exchange_pieces)),
+            pltpu.SemaphoreType.DMA((4, exchange_pieces)),
         ],
         input_output_aliases={4: 0},
         compiler_params=params(24),
@@ -723,21 +787,20 @@
     grain_substance_label,
     exchange_factor,
 ):
-    left, right, low, high, state = edges(gaseous_rho, gaseous_flow_vector, gaseous_kelvin)
-
-    def shifted(array, axis, step):
-        count = lax.axis_size(axis)
-        return lax.ppermute(array, axis, [(i, (i + step) % count) for i in range(count)])
-
+    left, right, x_one, x_two, y_one, y_two, state = edges(
+        gaseous_rho, gaseous_flow_vector, gaseous_kelvin
+    )
     received = (
-        shifted(right, "gx", 1),
-        shifted(left, "gx", -1),
-        shifted(high, "gy", 1),
-        shifted(low, "gy", -1),
-    )
-    shared, solid = binning(
+        swapped(x_one, "gx", False),
+        swapped(x_two, "gx", True),
+        swapped(y_one, "gy", False),
+        swapped(y_two, "gy", True),
+    )
+    shared, packed, solid = binning(
         bin_active_number,
         exchange_factor,
+        receiver_arrival_rank,
+        sender_tile_map.shape[1],
         grain_inertia,
         grain_motion_vector,
         grain_kelvin,
@@ -745,7 +808,7 @@
         grain_substance_label,
     )
     send, kept = occupied(
-        sender_tile_map, receiver_arrival_rank, state, (left, right), received, shared
+        sender_tile_map, state, (left, right), received, packed
     )
     devices = lax.axis_size("gx") * lax.axis_size("gy")
     width = send.shape[-1]

time: 56.9 us -> 55.5 us (0.975)
  Pallas kernels: 27.3 us -> 26 us
  waiting for transfers between devices: 14.3 us -> 13.4 us
  starting transfers between devices: 14.2 us -> 15 us
    ppermute x4, starting transfers between devices: 8.64 us -> 10.3 us  [swapped(): return lax.ppermute(array, axis, pairs)]
    ppermute x4, waiting for transfers between devices: 0.93 us -> 0.01 us  [swapped(): return lax.ppermute(array, axis, pairs)]
    all_to_all x1, starting transfers between devices: 5.52 us -> 4.78 us  [per_device(): lax.all_to_all(send.reshape(devices, block_rows, -1, width), ('gx', 'gy')...]
    pallas_call x1, Pallas kernels: 5.45 us -> 4.75 us  [exchange(): pl.pallas_call(exchange_kernel, out_shape=(pltpu.HBM(advanced.shape, jnp....]
    pallas_call x1, Pallas kernels: 5.15 us -> 4.55 us  [occupied(): pl.pallas_call(occupied_kernel, out_shape=(pltpu.HBM((total * block_rows,...]
  transfers between devices with their start and end apart: 5 -> 5, of which waited for: 2 -> 1; matrix products, arithmetic and copies ran while one was open for 0% -> 0% of each run, Pallas kernels for 24% -> 25%
where the time goes in v3:
time: 55.5 us; the launch traced here: 55.3 us
  Pallas kernels  26 us (47%)
  starting transfers between devices  15 us (27%)
  waiting for transfers between devices  13.4 us (24%)
  between operations  0.81 us (1%)
    all_to_all x1, waiting for transfers between devices, per_device(): lax.all_to_all(send.reshape(devices, block_rows, -1, width), ('gx', 'gy')...  13.4 us
    ppermute x4, starting transfers between devices, swapped(): return lax.ppermute(array, axis, pairs)  10.3 us
    pallas_call x1, Pallas kernels, advect(): pl.pallas_call(advect_kernel, out_shape=pltpu.HBM((fields, depth, height,...  9.73 us
    all_to_all x1, starting transfers between devices, per_device(): lax.all_to_all(send.reshape(devices, block_rows, -1, width), ('gx', 'gy')...  4.78 us
    pallas_call x1, Pallas kernels, exchange(): pl.pallas_call(exchange_kernel, out_shape=(pltpu.HBM(advanced.shape, jnp....  4.75 us
    pallas_call x1, Pallas kernels, occupied(): pl.pallas_call(occupied_kernel, out_shape=(pltpu.HBM((total * block_rows,...  4.55 us
    pallas_call x1, Pallas kernels, binning(): pl.pallas_call(binning_kernel, out_shape=(struct(6 * slots, lanes), struc...  3.95 us
    pallas_call x1, Pallas kernels, edges(): pl.pallas_call(edges_kernel, out_shape=(struct(height, width), struct(hei...  2.99 us
  transfers between devices with their start and end apart: 5, of which 1 were waited for; matrix products, arithmetic and copies ran while one was open for 0% of the time, Pallas kernels for 25%

profile of v3, /device:TPU:0, one launch (start us, length us, event | category | flops | bytes accessed | tf_op | source)
XLA Modules:
  0.0 55.3 jit_solution(9456931127903490443)
XLA Ops:
  0.6 0.0 copy-start.1
  0.6 0.0 copy-start.7
  0.7 0.0 copy-start.6
  0.7 0.0 copy-start.5
  0.7 0.0 copy-start.4
  0.7 0.0 copy-start.2
  0.7 0.0 copy-start.3
  0.7 0.0 copy-start.8
  0.7 3.0 %edges.1 = (f32[96,128]{1,0:T(8,128)S(1)}, f32[96,128]{1,0:T(8,128)S(1)}, f32[96,128]{1,0:T(8,128)S(1)}, f32[96,128]{1,0:T(8,128)S(1)}, f32[80,128]{1,0:T(8,128)...) custom-call(f32[16,96,128]{2,1,0:T(8,128)} %rho.3, f32[3,16,96,128]{3,2,1,0:T(8,128)} %flow.5, ...), custom_call_target="tpu_custom_call" | custom-call | tf_op jit(solution)/shard_map/edges/pallas_call | solution.py:121
  3.7 1.7 %collective-permute-start.2 = (f32[80,128]{1,0:T(8,128)S(1)}, f32[80,128]{1,0:T(8,128)S(1)}, u32[]{:S(2)}, u32[]{:S(2)}) collective-permute-start(f32[80,128]{1,0:T(8,128)S(1)} %get-tuple-element.21), channel_id=1, source_target_pairs={{0,1},{1,0},{2,3},{3,2},{4,5},{5,4},{6,7},{7,6},{8,9},{9,8},{10,11... | collective-permute-start | bytes 122888 | tf_op jit(solution)/shard_map/ppermute | solution.py:57
  5.5 4.4 %collective-permute-start.3 = (f32[80,128]{1,0:T(8,128)S(1)}, f32[80,128]{1,0:T(8,128)S(1)}, u32[]{:S(2)}, u32[]{:S(2)}) collective-permute-start(f32[80,128]{1,0:T(8,128)S(1)} %get-tuple-element.22), channel_id=1, source_target_pairs={{1,2},{2,1},{3,4},{4,3},{5,6},{6,5},{7,8},{8,7},{9,10},{10,9},{11,... | collective-permute-start | bytes 122888 | tf_op jit(solution)/shard_map/ppermute | solution.py:57
  9.8 0.0 collective-permute-start
  9.8 0.0 copy-start
  9.8 4.1 %collective-permute-start.1 = (f32[96,128]{1,0:T(8,128)S(1)}, f32[96,128]{1,0:T(8,128)S(1)}, u32[]{:S(2)}, u32[]{:S(2)}) collective-permute-start(f32[96,128]{1,0:T(8,128)S(1)} %get-tuple-element.20), channel_id=1, source_target_pairs={{16,32},{32,16},{48,64},{64,48},{80,96},{96,80},{112,0},{0,112},{1... | collective-permute-start | bytes 147464 | tf_op jit(solution)/shard_map/ppermute | solution.py:57
  14.0 0.0 copy-done.1
  14.0 0.0 copy-done.7
  14.0 0.0 copy-done.6
  14.0 0.0 copy-done.5
  14.0 0.0 copy-done.4
  14.0 0.0 copy-done.2
  14.0 0.0 copy-done.3
  14.0 0.0 copy-done.8
  14.0 4.0 %binning.1 = (f32[384,128]{1,0:T(8,128)S(1)}, f32[6,256,128]{2,1,0:T(8,128)S(1)}, f32[768,128]{1,0:T(8,128)S(1)}) custom-call(s32[64]{0:T(128)S(1)} %copy-done.8, f32[2,2]{1,0:T(2,128)S(1)} %copy-done.7, s32[64]{0:T(128)S(1)} %copy-done.1, f32[64,512]{1,0:T(8,128)S(1)} %copy-done.3, f32[3,64,512]{2,1,0:T(8,128)S(1)} %copy-done.2, f32[64,512]{1,0:T(8,128)S(1)} %copy-done.4, ...), custom_call_target="tpu_custom_call" | custom-call | flops 4000000000 | bytes 12000000 | tf_op jit(solution)/shard_map/binning/pallas_call | solution.py:223
  18.0 0.0 collective-permute-done.2.y_one
  18.0 0.0 collective-permute-done.3.y_two
  18.0 0.0 collective-permute-done.x_one
  18.0 0.0 collective-permute-done.1.x_two
  18.0 0.0 copy-done
  18.0 4.6 %occupied.1 = (f32[2816,128]{1,0:T(8,128)}, f32[5,256,128]{2,1,0:T(8,128)S(1)}, f32[5,2016,128]{2,1,0:T(8,128)S(1)}) custom-call(s32[1,256]{1,0:T(1,128)S(1)} %copy-done, f32[5,2016,128]{2,1,0:T(8,128)S(1)} %bitcast.5, f32[96,128]{1,0:T(8,128)S(1)} %get-tuple-element.17.own_left, ...), custom_call_target="tpu_custom_call", output_to_operand_aliasing={{2}: (1, {})} | custom-call | tf_op jit(solution)/shard_map/occupied/pallas_call | solution.py:427
  22.6 4.8 %all-to-all-start = ((f32[128,11,2,128]{3,2,1,0:T(2,128)}), f32[128,11,2,128]{3,2,1,0:T(2,128)S(1)}, u32[]{:S(2)}, u32[]{:S(2)}) async-start(f32[128,11,2,128]{3,2,1,0:T(2,128)} %bitcast.6), calls=%async_computation | async-start | bytes 2883584 | tf_op jit(solution)/shard_map/all_to_all | solution.py:815
  27.4 9.7 %advect.1.advanced = f32[5,16,96,128]{3,2,1,0:T(8,128)} custom-call(f32[16,96,128]{2,1,0:T(8,128)} %rho.3, f32[3,16,96,128]{3,2,1,0:T(8,128)} %flow.5, f32[16,96,128]{2,1,0:T(8,128)} %kelvin.5, f32[96,128]{1,0:T(8,128)S(1)} %get-tuple-element.17.own_left, f32[96,128]{1,0:T(8,128)S(1)} %get-tuple-element.18.own_right, ...), custom_call_target="tpu_custom_call" | custom-call | flops 4000000000 | bytes 12000000 | tf_op jit(solution)/shard_map/advect/pallas_call | solution.py:623
  37.1 13.4 %all-to-all-done = f32[128,11,2,128]{3,2,1,0:T(2,128)S(1)} async-done(((f32[128,11,2,128]{3,2,1,0:T(2,128)}), f32[128,11,2,128]{3,2,1,0:T(2,128)S(1)}, u32[]{:S(2)}, u32[]{:S(2)}) %all-to-all-start) | async-done | bytes 1441824 | tf_op jit(solution)/shard_map/all_to_all | solution.py:815
  50.5 4.8 %exchange.1 = (f32[5,16,96,128]{3,2,1,0:T(8,128)}, f32[4,128,128]{2,1,0:T(8,128)}) custom-call(s32[1,256]{1,0:T(1,128)S(1)} %copy-done, s32[64]{0:T(128)S(1)} %copy-done.1, f32[2816,128]{1,0:T(8,128)S(1)} %bitcast.4, f32[5,256,128]{2,1,0:T(8,128)S(1)} %get-tuple-element.25.kept, f32[5,16,96,128]{3,2,1,0:T(8,128)} %advect.1.advanced, ...), custom_call_target="tpu_custom_call", output_to_operand_aliasing={{0}: (4, {})} | custom-call | tf_op jit(solution)/shard_map/exchange/pallas_call | solution.py:758
Async XLA Ops:
  0.6 13.4 %copy-start.1 = (s32[64]{0:T(128)S(1)}, s32[64]{0:T(128)}, u32[]{:S(2)}) copy-start(s32[64]{0:T(128)} %rank.3) | copy-start | bytes 772
  0.6 13.3 %copy-start.7 = (f32[2,2]{1,0:T(2,128)S(1)}, f32[2,2]{1,0:T(2,128)}, u32[]{:S(2)}) copy-start(f32[2,2]{1,0:T(2,128)} %factor.1) | copy-start | bytes 52
  0.7 13.3 %copy-start.6 = (s32[64,512]{1,0:T(8,128)S(1)}, s32[64,512]{1,0:T(8,128)}, u32[]{:S(2)}) copy-start(s32[64,512]{1,0:T(8,128)} %label.1) | copy-start | bytes 393220
  0.7 13.3 %copy-start.5 = (s32[64,512]{1,0:T(8,128)S(1)}, s32[64,512]{1,0:T(8,128)}, u32[]{:S(2)}) copy-start(s32[64,512]{1,0:T(8,128)} %cell.1) | copy-start | bytes 393220
  0.7 13.3 %copy-start.4 = (f32[64,512]{1,0:T(8,128)S(1)}, f32[64,512]{1,0:T(8,128)}, u32[]{:S(2)}) copy-start(f32[64,512]{1,0:T(8,128)} %kelvin.4) | copy-start | bytes 393220
  0.7 13.3 %copy-start.2 = (f32[3,64,512]{2,1,0:T(8,128)S(1)}, f32[3,64,512]{2,1,0:T(8,128)}, u32[]{:S(2)}) copy-start(f32[3,64,512]{2,1,0:T(8,128)} %flow.4) | copy-start | bytes 1179652
  0.7 13.3 %copy-start.3 = (f32[64,512]{1,0:T(8,128)S(1)}, f32[64,512]{1,0:T(8,128)}, u32[]{:S(2)}) copy-start(f32[64,512]{1,0:T(8,128)} %mass.1) | copy-start | bytes 393220
  0.7 13.3 %copy-start.8 = (s32[64]{0:T(128)S(1)}, s32[64]{0:T(128)}, u32[]{:S(2)}) copy-start(s32[64]{0:T(128)} %count.1) | copy-start | bytes 772
  3.7 14.3 %collective-permute-start.2 = (f32[80,128]{1,0:T(8,128)S(1)}, f32[80,128]{1,0:T(8,128)S(1)}, u32[]{:S(2)}, u32[]{:S(2)}) collective-permute-start(f32[80,128]{1,0:T(8,128)S(1)} %get-tuple-element.21), channel_id=1, source_target_pairs={{0,1},{1,0},{2,3},{3,2},{4,5},{5,4},{6,7},{7,6},{8,9},{9,8},{10,11... | collective-permute-start | bytes 122888 | tf_op jit(solution)/shard_map/ppermute | solution.py:57
  5.5 12.6 %collective-permute-start.3 = (f32[80,128]{1,0:T(8,128)S(1)}, f32[80,128]{1,0:T(8,128)S(1)}, u32[]{:S(2)}, u32[]{:S(2)}) collective-permute-start(f32[80,128]{1,0:T(8,128)S(1)} %get-tuple-element.22), channel_id=1, source_target_pairs={{1,2},{2,1},{3,4},{4,3},{5,6},{6,5},{7,8},{8,7},{9,10},{10,9},{11,... | collective-permute-start | bytes 122888 | tf_op jit(solution)/shard_map/ppermute | solution.py:57
  9.8 8.2 %collective-permute-start = (f32[96,128]{1,0:T(8,128)S(1)}, f32[96,128]{1,0:T(8,128)S(1)}, u32[]{:S(2)}, u32[]{:S(2)}) collective-permute-start(f32[96,128]{1,0:T(8,128)S(1)} %get-tuple-element.19), channel_id=1, source_target_pairs={{0,16},{16,0},{32,48},{48,32},{64,80},{80,64},{96,112},{112,96},{1... | collective-permute-start | bytes 147464 | tf_op jit(solution)/shard_map/ppermute | solution.py:57
  9.8 8.2 %copy-start = (s32[1,256]{1,0:T(1,128)S(1)}, s32[1,256]{1,0:T(1,128)}, u32[]{:S(2)}) copy-start(s32[1,256]{1,0:T(1,128)} %tiles.3) | copy-start | bytes 3076
  9.8 8.2 %collective-permute-start.1 = (f32[96,128]{1,0:T(8,128)S(1)}, f32[96,128]{1,0:T(8,128)S(1)}, u32[]{:S(2)}, u32[]{:S(2)}) collective-permute-start(f32[96,128]{1,0:T(8,128)S(1)} %get-tuple-element.20), channel_id=1, source_target_pairs={{16,32},{32,16},{48,64},{64,48},{80,96},{96,80},{112,0},{0,112},{1... | collective-permute-start | bytes 147464 | tf_op jit(solution)/shard_map/ppermute | solution.py:57
  22.6 27.9 %all-to-all-start = ((f32[128,11,2,128]{3,2,1,0:T(2,128)}), f32[128,11,2,128]{3,2,1,0:T(2,128)S(1)}, u32[]{:S(2)}, u32[]{:S(2)}) async-start(f32[128,11,2,128]{3,2,1,0:T(2,128)} %bitcast.6), calls=%async_computation | async-start | bytes 2883584 | tf_op jit(solution)/shard_map/all_to_all | solution.py:815

commit v4 on v3

--- a/solution.py
+++ b/solution.py
@@ -61,7 +61,7 @@
     depth, height, _ = rho.shape
     parts = sems.shape[1]
     planes = depth // parts
-    rows = 24
+    rows = 48
     inner = pl.ds(row_pad, height)
 
     def copies(part):
@@ -181,7 +181,7 @@
         sums[pl.ds(pl.multiple_of(s * 16, 16), 16), :] = summed[0:16] + summed[16:32]
         return carry
 
-    lax.fori_loop(0, slots, slot_sums, 0, unroll=32)
+    lax.fori_loop(0, slots, slot_sums, 0, unroll=64)
     totals = [0.0] * 6
     for m in range(2):
         drag, thermal = factor[m, 0], factor[m, 1]

time: 55.5 us -> 55.2 us (level)
  no operation moved by 1% of the time
where the time goes in v4:
time: 55.2 us; the launch traced here: 55 us
  Pallas kernels  25.8 us (47%)
  starting transfers between devices  14.9 us (27%)
  waiting for transfers between devices  13.4 us (24%)
  between operations  0.81 us (1%)
    all_to_all x1, waiting for transfers between devices, per_device(): lax.all_to_all(send.reshape(devices, block_rows, -1, width), ('gx', 'gy')...  13.4 us
    ppermute x4, starting transfers between devices, swapped(): return lax.ppermute(array, axis, pairs)  10.3 us
    pallas_call x1, Pallas kernels, advect(): pl.pallas_call(advect_kernel, out_shape=pltpu.HBM((fields, depth, height,...  9.73 us
    pallas_call x1, Pallas kernels, exchange(): pl.pallas_call(exchange_kernel, out_shape=(pltpu.HBM(advanced.shape, jnp....  4.75 us
    all_to_all x1, starting transfers between devices, per_device(): lax.all_to_all(send.reshape(devices, block_rows, -1, width), ('gx', 'gy')...  4.65 us
    pallas_call x1, Pallas kernels, occupied(): pl.pallas_call(occupied_kernel, out_shape=(pltpu.HBM((total * block_rows,...  4.55 us
    pallas_call x1, Pallas kernels, binning(): pl.pallas_call(binning_kernel, out_shape=(struct(6 * slots, lanes), struc...  3.87 us
    pallas_call x1, Pallas kernels, edges(): pl.pallas_call(edges_kernel, out_shape=(struct(height, width), struct(hei...  2.94 us
  transfers between devices with their start and end apart: 5, of which 1 were waited for; matrix products, arithmetic and copies ran while one was open for 0% of the time, Pallas kernels for 25%

profile of v4, /device:TPU:0, one launch (start us, length us, event | category | flops | bytes accessed | tf_op | source)
XLA Modules:
  0.0 55.0 jit_solution(10854034405181826800)
XLA Ops:
  0.6 0.0 copy-start.1
  0.6 0.0 copy-start.7
  0.7 0.0 copy-start.6
  0.7 0.0 copy-start.5
  0.7 0.0 copy-start.4
  0.7 0.0 copy-start.2
  0.7 0.0 copy-start.3
  0.7 0.0 copy-start.8
  0.7 2.9 %edges.1 = (f32[96,128]{1,0:T(8,128)S(1)}, f32[96,128]{1,0:T(8,128)S(1)}, f32[96,128]{1,0:T(8,128)S(1)}, f32[96,128]{1,0:T(8,128)S(1)}, f32[80,128]{1,0:T(8,128)...) custom-call(f32[16,96,128]{2,1,0:T(8,128)} %rho.3, f32[3,16,96,128]{3,2,1,0:T(8,128)} %flow.5, ...), custom_call_target="tpu_custom_call" | custom-call | tf_op jit(solution)/shard_map/edges/pallas_call | solution.py:121
  3.7 1.7 %collective-permute-start.2 = (f32[80,128]{1,0:T(8,128)S(1)}, f32[80,128]{1,0:T(8,128)S(1)}, u32[]{:S(2)}, u32[]{:S(2)}) collective-permute-start(f32[80,128]{1,0:T(8,128)S(1)} %get-tuple-element.21), channel_id=1, source_target_pairs={{0,1},{1,0},{2,3},{3,2},{4,5},{5,4},{6,7},{7,6},{8,9},{9,8},{10,11... | collective-permute-start | bytes 122888 | tf_op jit(solution)/shard_map/ppermute | solution.py:57
  5.4 4.4 %collective-permute-start.3 = (f32[80,128]{1,0:T(8,128)S(1)}, f32[80,128]{1,0:T(8,128)S(1)}, u32[]{:S(2)}, u32[]{:S(2)}) collective-permute-start(f32[80,128]{1,0:T(8,128)S(1)} %get-tuple-element.22), channel_id=1, source_target_pairs={{1,2},{2,1},{3,4},{4,3},{5,6},{6,5},{7,8},{8,7},{9,10},{10,9},{11,... | collective-permute-start | bytes 122888 | tf_op jit(solution)/shard_map/ppermute | solution.py:57
  9.8 0.0 collective-permute-start
  9.8 0.0 copy-start
  9.8 4.1 %collective-permute-start.1 = (f32[96,128]{1,0:T(8,128)S(1)}, f32[96,128]{1,0:T(8,128)S(1)}, u32[]{:S(2)}, u32[]{:S(2)}) collective-permute-start(f32[96,128]{1,0:T(8,128)S(1)} %get-tuple-element.20), channel_id=1, source_target_pairs={{16,32},{32,16},{48,64},{64,48},{80,96},{96,80},{112,0},{0,112},{1... | collective-permute-start | bytes 147464 | tf_op jit(solution)/shard_map/ppermute | solution.py:57
  13.9 0.0 copy-done.1
  13.9 0.0 copy-done.7
  13.9 0.0 copy-done.6
  13.9 0.0 copy-done.5
  13.9 0.0 copy-done.4
  13.9 0.0 copy-done.2
  14.0 0.0 copy-done.3
  14.0 0.0 copy-done.8
  14.0 3.9 %binning.1 = (f32[384,128]{1,0:T(8,128)S(1)}, f32[6,256,128]{2,1,0:T(8,128)S(1)}, f32[768,128]{1,0:T(8,128)S(1)}) custom-call(s32[64]{0:T(128)S(1)} %copy-done.8, f32[2,2]{1,0:T(2,128)S(1)} %copy-done.7, s32[64]{0:T(128)S(1)} %copy-done.1, f32[64,512]{1,0:T(8,128)S(1)} %copy-done.3, f32[3,64,512]{2,1,0:T(8,128)S(1)} %copy-done.2, f32[64,512]{1,0:T(8,128)S(1)} %copy-done.4, ...), custom_call_target="tpu_custom_call" | custom-call | flops 4000000000 | bytes 12000000 | tf_op jit(solution)/shard_map/binning/pallas_call | solution.py:223
  17.9 0.0 collective-permute-done.2.y_one
  17.9 0.0 collective-permute-done.3.y_two
  17.9 0.0 collective-permute-done.x_one
  17.9 0.0 collective-permute-done.1.x_two
  17.9 0.0 copy-done
  17.9 4.6 %occupied.1 = (f32[2816,128]{1,0:T(8,128)}, f32[5,256,128]{2,1,0:T(8,128)S(1)}, f32[5,2016,128]{2,1,0:T(8,128)S(1)}) custom-call(s32[1,256]{1,0:T(1,128)S(1)} %copy-done, f32[5,2016,128]{2,1,0:T(8,128)S(1)} %bitcast.5, f32[96,128]{1,0:T(8,128)S(1)} %get-tuple-element.17.own_left, ...), custom_call_target="tpu_custom_call", output_to_operand_aliasing={{2}: (1, {})} | custom-call | tf_op jit(solution)/shard_map/occupied/pallas_call | solution.py:427
  22.5 4.7 %all-to-all-start = ((f32[128,11,2,128]{3,2,1,0:T(2,128)}), f32[128,11,2,128]{3,2,1,0:T(2,128)S(1)}, u32[]{:S(2)}, u32[]{:S(2)}) async-start(f32[128,11,2,128]{3,2,1,0:T(2,128)} %bitcast.6), calls=%async_computation | async-start | bytes 2883584 | tf_op jit(solution)/shard_map/all_to_all | solution.py:815
  27.1 9.7 %advect.1.advanced = f32[5,16,96,128]{3,2,1,0:T(8,128)} custom-call(f32[16,96,128]{2,1,0:T(8,128)} %rho.3, f32[3,16,96,128]{3,2,1,0:T(8,128)} %flow.5, f32[16,96,128]{2,1,0:T(8,128)} %kelvin.5, f32[96,128]{1,0:T(8,128)S(1)} %get-tuple-element.17.own_left, f32[96,128]{1,0:T(8,128)S(1)} %get-tuple-element.18.own_right, ...), custom_call_target="tpu_custom_call" | custom-call | flops 4000000000 | bytes 12000000 | tf_op jit(solution)/shard_map/advect/pallas_call | solution.py:623
  36.9 13.4 %all-to-all-done = f32[128,11,2,128]{3,2,1,0:T(2,128)S(1)} async-done(((f32[128,11,2,128]{3,2,1,0:T(2,128)}), f32[128,11,2,128]{3,2,1,0:T(2,128)S(1)}, u32[]{:S(2)}, u32[]{:S(2)}) %all-to-all-start) | async-done | bytes 1441824 | tf_op jit(solution)/shard_map/all_to_all | solution.py:815
  50.2 4.8 %exchange.1 = (f32[5,16,96,128]{3,2,1,0:T(8,128)}, f32[4,128,128]{2,1,0:T(8,128)}) custom-call(s32[1,256]{1,0:T(1,128)S(1)} %copy-done, s32[64]{0:T(128)S(1)} %copy-done.1, f32[2816,128]{1,0:T(8,128)S(1)} %bitcast.4, f32[5,256,128]{2,1,0:T(8,128)S(1)} %get-tuple-element.25.kept, f32[5,16,96,128]{3,2,1,0:T(8,128)} %advect.1.advanced, ...), custom_call_target="tpu_custom_call", output_to_operand_aliasing={{0}: (4, {})} | custom-call | tf_op jit(solution)/shard_map/exchange/pallas_call | solution.py:758
Async XLA Ops:
  0.6 13.3 %copy-start.1 = (s32[64]{0:T(128)S(1)}, s32[64]{0:T(128)}, u32[]{:S(2)}) copy-start(s32[64]{0:T(128)} %rank.3) | copy-start | bytes 772
  0.6 13.3 %copy-start.7 = (f32[2,2]{1,0:T(2,128)S(1)}, f32[2,2]{1,0:T(2,128)}, u32[]{:S(2)}) copy-start(f32[2,2]{1,0:T(2,128)} %factor.1) | copy-start | bytes 52
  0.7 13.3 %copy-start.6 = (s32[64,512]{1,0:T(8,128)S(1)}, s32[64,512]{1,0:T(8,128)}, u32[]{:S(2)}) copy-start(s32[64,512]{1,0:T(8,128)} %label.1) | copy-start | bytes 393220
  0.7 13.3 %copy-start.5 = (s32[64,512]{1,0:T(8,128)S(1)}, s32[64,512]{1,0:T(8,128)}, u32[]{:S(2)}) copy-start(s32[64,512]{1,0:T(8,128)} %cell.1) | copy-start | bytes 393220
  0.7 13.3 %copy-start.4 = (f32[64,512]{1,0:T(8,128)S(1)}, f32[64,512]{1,0:T(8,128)}, u32[]{:S(2)}) copy-start(f32[64,512]{1,0:T(8,128)} %kelvin.4) | copy-start | bytes 393220
  0.7 13.3 %copy-start.2 = (f32[3,64,512]{2,1,0:T(8,128)S(1)}, f32[3,64,512]{2,1,0:T(8,128)}, u32[]{:S(2)}) copy-start(f32[3,64,512]{2,1,0:T(8,128)} %flow.4) | copy-start | bytes 1179652
  0.7 13.3 %copy-start.3 = (f32[64,512]{1,0:T(8,128)S(1)}, f32[64,512]{1,0:T(8,128)}, u32[]{:S(2)}) copy-start(f32[64,512]{1,0:T(8,128)} %mass.1) | copy-start | bytes 393220
  0.7 13.3 %copy-start.8 = (s32[64]{0:T(128)S(1)}, s32[64]{0:T(128)}, u32[]{:S(2)}) copy-start(s32[64]{0:T(128)} %count.1) | copy-start | bytes 772
  3.7 14.2 %collective-permute-start.2 = (f32[80,128]{1,0:T(8,128)S(1)}, f32[80,128]{1,0:T(8,128)S(1)}, u32[]{:S(2)}, u32[]{:S(2)}) collective-permute-start(f32[80,128]{1,0:T(8,128)S(1)} %get-tuple-element.21), channel_id=1, source_target_pairs={{0,1},{1,0},{2,3},{3,2},{4,5},{5,4},{6,7},{7,6},{8,9},{9,8},{10,11... | collective-permute-start | bytes 122888 | tf_op jit(solution)/shard_map/ppermute | solution.py:57
  5.4 12.5 %collective-permute-start.3 = (f32[80,128]{1,0:T(8,128)S(1)}, f32[80,128]{1,0:T(8,128)S(1)}, u32[]{:S(2)}, u32[]{:S(2)}) collective-permute-start(f32[80,128]{1,0:T(8,128)S(1)} %get-tuple-element.22), channel_id=1, source_target_pairs={{1,2},{2,1},{3,4},{4,3},{5,6},{6,5},{7,8},{8,7},{9,10},{10,9},{11,... | collective-permute-start | bytes 122888 | tf_op jit(solution)/shard_map/ppermute | solution.py:57
  9.8 8.1 %collective-permute-start = (f32[96,128]{1,0:T(8,128)S(1)}, f32[96,128]{1,0:T(8,128)S(1)}, u32[]{:S(2)}, u32[]{:S(2)}) collective-permute-start(f32[96,128]{1,0:T(8,128)S(1)} %get-tuple-element.19), channel_id=1, source_target_pairs={{0,16},{16,0},{32,48},{48,32},{64,80},{80,64},{96,112},{112,96},{1... | collective-permute-start | bytes 147464 | tf_op jit(solution)/shard_map/ppermute | solution.py:57
  9.8 8.1 %copy-start = (s32[1,256]{1,0:T(1,128)S(1)}, s32[1,256]{1,0:T(1,128)}, u32[]{:S(2)}) copy-start(s32[1,256]{1,0:T(1,128)} %tiles.3) | copy-start | bytes 3076
  9.8 8.1 %collective-permute-start.1 = (f32[96,128]{1,0:T(8,128)S(1)}, f32[96,128]{1,0:T(8,128)S(1)}, u32[]{:S(2)}, u32[]{:S(2)}) collective-permute-start(f32[96,128]{1,0:T(8,128)S(1)} %get-tuple-element.20), channel_id=1, source_target_pairs={{16,32},{32,16},{48,64},{64,48},{80,96},{96,80},{112,0},{0,112},{1... | collective-permute-start | bytes 147464 | tf_op jit(solution)/shard_map/ppermute | solution.py:57
  22.5 27.8 %all-to-all-start = ((f32[128,11,2,128]{3,2,1,0:T(2,128)}), f32[128,11,2,128]{3,2,1,0:T(2,128)S(1)}, u32[]{:S(2)}, u32[]{:S(2)}) async-start(f32[128,11,2,128]{3,2,1,0:T(2,128)} %bitcast.6), calls=%async_computation | async-start | bytes 2883584 | tf_op jit(solution)/shard_map/all_to_all | solution.py:815
